TPU v7x, 512 devices: a whole 4x8x8 slice. The times are simulated.
512 devices in a mesh: row: 16 (over x_hi, z), col: 32 (over y, x_lo, core).
Axes of the slice: x: 4 (x_hi: 2, x_lo: 2; x = x_hi * 2 + x_lo), y: 8, z: 8, core: 2. Of those that a mesh axis runs over, the one named last changes fastest.
Arguments:
- points: float32 [64, 65536], P(None, ('row', 'col')), may hold values from -6 to 6
- targets: float32 [65536], P(('row', 'col')), may hold values from -6 to 6
- probes: float32 [32, 65536], P(None, ('row', 'col')), may hold values from -6 to 6
- lengthscale: float32 [1], replicated, may hold values from 3.5 to 5
- outputscale: float32 [1], replicated, may hold values from 0.5 to 2
- noise: float32 [1], replicated, may hold values from 0.05 to 0.5
Outputs:
- solution: float32 [33, 65536], P(None, ('row', 'col'))
- residual: float32 [33, 65536], P(None, ('row', 'col'))
- direction: float32 [33, 65536], P(None, ('row', 'col'))
- length_products: float32 [32, 65536], P(None, ('row', 'col'))
- scale_products: float32 [32, 65536], P(None, ('row', 'col'))
All inputs are finite; a program needn't handle non-finite values.
Results may differ from a plain program's by a relative error of at most 0.0003.
Values sent between devices are 32-bit elements; how exact they have to be, the bound alone decides.
No kernel may reach another device: no remote copies, remote signals or barrier semaphores. Data moves between devices by JAX's collectives and lax.ppermute only.
A program may use at most 64 MiB of HBM per device.

v0:
```python
import jax
import jax.numpy as jnp
from jax import lax
from jax.sharding import PartitionSpec as P


def make_fold(row_x, width, inv_two, n_rhs, n_probes):
    sq_rows = jnp.sum(row_x * row_x, axis=0)
    n_rows = row_x.shape[1]
    feats = row_x.shape[0]

    def accumulate(carry, pieces, start):
        col_x, col_rhs = pieces
        count = col_x.shape[1] // width
        xs = jnp.transpose(col_x.reshape(feats, count, width), (1, 0, 2))
        bs = jnp.transpose(col_rhs.reshape(n_rhs, count, width), (1, 0, 2))

        def step(totals, item):
            x_block, b_block = item
            sq_cols = jnp.sum(x_block * x_block, axis=0)
            dots = lax.dot_general(
                x_block,
                row_x,
                (((0,), (0,)), ((), ())),
                precision=lax.Precision.HIGHEST,
                preferred_element_type=jnp.float32,
            )
            dist = jnp.maximum(sq_cols[:, None] + sq_rows[None, :] - 2.0 * dots, 0.0)
            kern = jnp.exp(-dist * inv_two)
            eb_new = totals[0] + jnp.dot(
                b_block, kern, precision=lax.Precision.HIGHEST, preferred_element_type=jnp.float32
            )
            ed_new = totals[1] + jnp.dot(
                b_block[1:],
                kern * dist,
                precision=lax.Precision.HIGHEST,
                preferred_element_type=jnp.float32,
            )
            return ((eb_new, ed_new), None)

        result, unused = lax.scan(step, carry, (xs, bs))
        return result

    init = (jnp.zeros((n_rhs, n_rows), jnp.float32), jnp.zeros((n_probes, n_rows), jnp.float32))
    return (accumulate, init)


def shards(points, targets, probes, lengthscale, outputscale, noise):
    rhs = jnp.concatenate([targets[None, :], probes], 0)
    width = points.shape[1]
    n_rhs = rhs.shape[0]
    n_probes = probes.shape[0]
    inv_two = 0.5 / (lengthscale[0] * lengthscale[0])
    row_x = lax.all_gather(points, "col", axis=1, tiled=True)
    accumulate, init = make_fold(row_x, width, inv_two, n_rhs, n_probes)
    eb_part, ed_part = accumulate(
        init,
        (
            lax.all_gather(points, "row", axis=1, tiled=True),
            lax.all_gather(rhs, "row", axis=1, tiled=True),
        ),
        jnp.int32(0),
    )
    eb, ed = (
        lax.psum_scatter(eb_part, "col", scatter_dimension=1, tiled=True),
        lax.psum_scatter(ed_part, "col", scatter_dimension=1, tiled=True),
    )
    scale = outputscale[0]
    kb = scale * eb + noise[0] * rhs
    scale_products = eb[1:]
    length_products = scale / lengthscale[0] ** 3 * ed
    norm_old, curv = lax.psum(
        (jnp.sum(rhs * rhs, axis=1), jnp.sum(rhs * kb, axis=1)), ("row", "col")
    )
    alpha = norm_old / curv
    residual = rhs - alpha[:, None] * kb
    norm_new = lax.psum(jnp.sum(residual * residual, axis=1), ("row", "col"))
    solution = alpha[:, None] * rhs
    direction = residual + (norm_new / norm_old)[:, None] * rhs
    return (solution, residual, direction, length_products, scale_products)


def solution(mesh):
    placed = (P(None, ("row", "col")), P(("row", "col")), P(None, ("row", "col")), P(), P(), P())
    return jax.shard_map(
        shards,
        mesh=mesh,
        in_specs=placed,
        out_specs=(
            P(None, ("row", "col")),
            P(None, ("row", "col")),
            P(None, ("row", "col")),
            P(None, ("row", "col")),
            P(None, ("row", "col")),
        ),
        check_vma=False,
    )
```

profile of v0, /device:TPU:1, one launch (start us, length us, event | category | flops | bytes accessed | tf_op | source)
XLA Modules:
  0.0 681.7 jit_solution(353375499027567485)
XLA Ops:
  9.4 42.3 %all_gather.9 = f32[33,2048]{1,0:T(8,128)S(1)} all-gather(f32[33,128]{1,0:T(8,128)S(1)} %pad_maximum_fusion), channel_id=1, replica_groups=mesh['row'=16,'col'=32] {'row'}, dimensions={1}, use_global_device_ids=true | all-gather | bytes 287232 | tf_op jit(solution)/shard_map/all_gather | solution.py:60
  52.6 31.9 %all_gather.10 = f32[64,2048]{1,0:T(8,128)S(1)} all-gather(f32[64,128]{1,0:T(8,128)S(1)} %copy-done.3), channel_id=1, replica_groups=mesh['row'=16,'col'=32] {'row'}, dimensions={1}, use_global_device_ids=true | all-gather | bytes 557056 | tf_op jit(solution)/shard_map/all_gather | solution.py:59
  86.8 143.1 %while.13 = (s32[]{:T(128)}, f32[33,4096]{1,0:T(8,128)S(1)}, f32[32,4096]{1,0:T(8,128)S(1)}, f32[16,33,128]{2,1,0:T(8,128)}, f32[16,64,128]{2,0,1:T(8,128)}, /*i...) while((s32[]{:T(128)}, f32[33,4096]{1,0:T(8,128)S(1)}, ...), condition=%wide.region_5.6_spmd.clone, body=%wide.region_3.5_spmd.clone.sunk | while | flops 816865152 | bytes 9657484 | solution.py:41
  87.8 3.2 fusion.20
  96.8 3.2 fusion.20
  105.7 3.2 fusion.20
  109.0 2.3 convolution_add_fusion.4
  114.7 3.2 fusion.20
  117.9 2.3 convolution_add_fusion.4
  123.6 3.2 fusion.20
  132.6 3.2 fusion.20
  135.8 2.3 convolution_add_fusion.4
  141.5 3.2 fusion.20
  144.8 2.3 convolution_add_fusion.4
  150.5 3.2 fusion.20
  159.4 3.2 fusion.20
  162.7 2.3 convolution_add_fusion.4
  168.4 3.2 fusion.20
  171.6 2.3 convolution_add_fusion.4
  177.3 3.2 fusion.20
  186.2 3.2 fusion.20
  189.5 2.3 convolution_add_fusion.4
  195.2 3.2 fusion.20
  198.4 2.3 convolution_add_fusion.4
  204.1 3.2 fusion.20
  213.1 3.2 fusion.20
  216.3 2.3 convolution_add_fusion.4
  222.0 3.2 fusion.20
  232.8 122.8 %reduce-scatter.5.cloned.1.call-done = f32[32,128]{1,0:T(8,128)} async-done(((f32[32,4096]{1,0:T(8,128)}), f32[32,128]{1,0:T(8,128)}) %reduce-scatter.5.cloned.1.call-update) | async-done | bytes 16400 | tf_op jit(solution)/shard_map/reduce_scatter | solution.py:66
  357.0 119.5 %reduce-scatter.3.cloned.1.call-done = f32[33,128]{1,0:T(8,128)} async-done(((f32[33,4096]{1,0:T(8,128)}), f32[33,128]{1,0:T(8,128)}) %reduce-scatter.3.cloned.1.call-update) | async-done | bytes 16912 | tf_op jit(solution)/shard_map/reduce_scatter | solution.py:65
  477.4 99.8 %all-reduce = (f32[33]{0:T(128)S(1)}, f32[33]{0:T(128)S(1)}) all-reduce(f32[33]{0:T(128)S(1)} %get-tuple-element.86, f32[33]{0:T(128)S(1)} %get-tuple-element.85), channel_id=1, replica_groups=mesh['row'=16,'col'=32] {'row','col'}, use_global_device_ids=true, to_apply=%region_1.2 | all-reduce | flops 66 | bytes 528 | tf_op jit(solution)/shard_map/psum | solution.py:72
  578.7 94.4 %psum.23 = f32[33]{0:T(128)S(1)} all-reduce(f32[33]{0:T(128)S(1)} %get-tuple-element.105), channel_id=1, replica_groups=mesh['row'=16,'col'=32] {'row','col'}, use_global_device_ids=true, to_apply=%region_10.11 | all-reduce | flops 33 | bytes 264 | tf_op jit(solution)/shard_map/psum | solution.py:77
  (89 shorter events, 81.3 us)
Async XLA Ops:
  7.2 45.4 %copy-start.3 = (f32[64,128]{1,0:T(8,128)S(1)}, f32[64,128]{1,0:T(8,128)}, u32[]{:S(2)}) copy-start(f32[64,128]{1,0:T(8,128)} %param.8) | copy-start | bytes 98308
  7.2 78.3 %all-gather.2.cloned.1.call-start = ((), (), s32[]{:S(2)}) async-start(), calls=%async_computation.2 | async-start | bytes 1081344 | tf_op jit(solution)/shard_map/all_gather | solution.py:54
  7.9 347.8 %reduce-scatter.5.cloned.1.call-start = ((), (), s32[]{:S(2)}) async-start(), calls=%async_computation.4 | async-start | bytes 540672 | tf_op jit(solution)/shard_map/reduce_scatter | solution.py:66
  86.8 389.8 %copy-start.2 = (f32[32,128]{1,0:T(8,128)S(1)}, f32[32,128]{1,0:T(8,128)}, u32[]{:S(2)}) copy-start(f32[32,128]{1,0:T(8,128)} %param.10) | copy-start | bytes 49156
  86.8 389.7 %copy-start.5 = (f32[128]{0:T(128)S(1)}, f32[128]{0:T(128)}, u32[]{:S(2)}) copy-start(f32[128]{0:T(128)} %param.9) | copy-start | bytes 1540
  230.0 0.8 copy-start.1
  230.0 1.0 copy-start
  230.8 245.8 %reduce-scatter.3.cloned.1.call-start = ((), (), s32[]{:S(2)}) async-start(), calls=%async_computation.3 | async-start | bytes 675840 | tf_op jit(solution)/shard_map/reduce_scatter | solution.py:65
  578.7 96.5 %copy-start.4 = (f32[33,128]{1,0:T(8,128)}, f32[33,128]{1,0:T(8,128)S(1)}, u32[]{:S(2)}) copy-start(f32[33,128]{1,0:T(8,128)S(1)} %get-tuple-element.106) | copy-start | bytes 50692
Sparse Core Ops, SparseCore 0:
  10.1 70.9 all-gather.1
  230.9 124.7 reduce-scatter.4
  358.7 117.7 reduce-scatter.2
where the time goes:
time: 685 us; the launch traced here: 682 us
  blocking collectives  268 us (39%)
  waiting for transfers between devices  244 us (36%)
  matrix products  126 us (18%)
  local copies, waits for them, and re-layouts  19.8 us (3%)
  between operations  15.9 us (2%)
    reduce_scatter x1, waiting for transfers between devices, shards(): lax.psum_scatter(ed_part, 'col', scatter_dimension=1, tiled=True)  123 us
    reduce_scatter x1, waiting for transfers between devices, shards(): lax.psum_scatter(eb_part, 'col', scatter_dimension=1, tiled=True)  120 us
    psum x1, blocking collectives, shards(): lax.psum((jnp.sum(rhs * rhs, axis=1), jnp.sum(rhs * kb, axis=1)), ('row',...  99.8 us
    psum x1, blocking collectives, shards(): norm_new = lax.psum(jnp.sum(residual * residual, axis=1), ('row', 'col'))  94.4 us
    dot_general x16, matrix products, step(): lax.dot_general(x_block, row_x, (((0,), (0,)), ((), ())), precision=lax.P...  51.8 us
    all_gather x1, blocking collectives, shards(): lax.all_gather(rhs, 'row', axis=1, tiled=True)  42.3 us
    dot_general x16, matrix products, step(): jnp.dot(b_block, kern, precision=lax.Precision.HIGHEST, preferred_element...  37.5 us
    dot_general x16, matrix products, step(): jnp.dot(b_block[1:], kern * dist, precision=lax.Precision.HIGHEST, prefer...  36.9 us
  transfers between devices with their start and end apart: 3, of which 2 were waited for; matrix products, arithmetic and copies ran while one was open for 1% of the time, Pallas kernels for 0%

commit v1 on v0

v1 whole, which is shorter than its diff:
```python
import math

import jax
import jax.numpy as jnp
from jax import lax
from jax.experimental import pallas as pl
from jax.experimental.pallas import tpu as pltpu
from jax.sharding import Mesh, PartitionSpec as P

AXES = ("xh", "z", "y", "xl", "co")
SIZES = (2, 8, 8, 2, 2)
I_GROUP = ("y", "xl")
J_GROUP = ("xh", "z")
N_I = 16
N_J = 16
LANES = 128
F = 64
PROBES = 32
SENT = 104
BACK = 72
BI = 512
f32, bf16 = jnp.float32, jnp.bfloat16
LOG2E = math.log2(math.e)
VMEM = pl.BlockSpec(memory_space=pltpu.VMEM)
SMEM = pl.BlockSpec(memory_space=pltpu.SMEM)


def halves(x):
    hi = x.astype(bf16)
    return hi, (x - hi.astype(f32)).astype(bf16)


def tile(t, size=LANES):
    return pl.ds(pl.multiple_of(t * size, size), size)


def products_kernel(ls_ref, xi_ref, xa_ref, xb_ref, out_ref, left, sq_i, right, sq_j, rhs):
    rows = left.shape[1]
    ell = ls_ref[0]
    c = (0.5 * LOG2E) / (ell * ell)

    def prepare_i(t, unused):
        hi, lo = halves(xi_ref[t])
        x = hi.astype(f32) + lo.astype(f32)
        yh, yl = halves((2.0 * c) * x)
        at = tile(t)
        left[0:64, at] = yh
        left[64:128, at] = yl
        left[128:192, at] = yh
        left[192:256, at] = yl
        sq_i[:, at] = jnp.broadcast_to(-c * jnp.sum(x * x, axis=0, keepdims=True), (8, LANES))
        return unused

    lax.fori_loop(0, N_I, prepare_i, 0, unroll=4)

    def prepare_j(x_ref, first):
        def body(t, unused):
            hi, lo = halves(x_ref[t, 0:64])
            x = hi.astype(f32) + lo.astype(f32)
            at = tile(first + t)
            turned = jnp.concatenate([hi.astype(f32), lo.astype(f32)], axis=0).T.astype(bf16)
            right[at, 0:64] = turned[:, 0:64]
            right[at, 64:128] = turned[:, 0:64]
            right[at, 128:192] = turned[:, 64:128]
            right[at, 192:256] = turned[:, 64:128]
            sq = jnp.broadcast_to(-c * jnp.sum(x * x, axis=0, keepdims=True), (LANES, LANES))
            sq_j[at, :] = sq.T
            bh, bl = halves(x_ref[t, 64:104])
            rhs[0:40, at] = bh
            rhs[40:80, at] = bl
            return unused

        lax.fori_loop(0, N_J, body, 0, unroll=4)

    prepare_j(xa_ref, 0)
    prepare_j(xb_ref, N_J)

    def block(ib, unused):
        at = tile(ib, BI)
        dots = jnp.dot(right[...], left[:, at], preferred_element_type=f32)
        sq = jnp.concatenate([sq_j[...]] * (BI // LANES), axis=1)
        power = jnp.minimum(dots + sq_i[0:1, at] + sq, 0.0)
        kern = jnp.exp2(power)
        kh, kl = halves(kern)
        dh, dl = halves(kern * power)
        eb = jnp.dot(rhs[...], kh, preferred_element_type=f32)
        ed = jnp.dot(rhs[...], dh, preferred_element_type=f32)
        eb = eb[0:40] + eb[40:80] + jnp.dot(rhs[0:40], kl, preferred_element_type=f32)
        ed = ed[0:40] + ed[40:80] + jnp.dot(rhs[0:40], dl, preferred_element_type=f32)
        for p in range(BI // LANES):
            out_ref[ib * (BI // LANES) + p, 0:40] = eb[:, p * LANES : (p + 1) * LANES]
            out_ref[ib * (BI // LANES) + p, 40:72] = ed[0:32, p * LANES : (p + 1) * LANES]
        return unused

    lax.fori_loop(0, rows // BI, block, 0)


def products(lengthscale, xi, xa, xb):
    rows, cols = N_I * LANES, 2 * N_J * LANES
    return pl.pallas_call(
        products_kernel,
        out_shape=jax.ShapeDtypeStruct((N_I, BACK, LANES), f32),
        in_specs=[SMEM, VMEM, VMEM, VMEM],
        out_specs=VMEM,
        scratch_shapes=[
            pltpu.VMEM((256, rows), bf16),
            pltpu.VMEM((8, rows), f32),
            pltpu.VMEM((cols, 256), bf16),
            pltpu.VMEM((cols, LANES), f32),
            pltpu.VMEM((80, cols), bf16),
        ],
        compiler_params=pltpu.CompilerParams(vmem_limit_bytes=48 << 20),
        cost_estimate=pl.CostEstimate(flops=2 * rows * cols * 1024, bytes_accessed=4 << 20, transcendentals=rows * cols),
        name="products",
    )(lengthscale, xi, xa, xb)


def sums_kernel(ls_ref, os_ref, own_ref, part_ref, lp_ref, sp_ref, off_ref, stat_ref):
    total = part_ref[0]
    for s in range(1, N_I):
        total = total + part_ref[s]
    eb = total[0:40]
    sp_ref[...] = eb[0:32]
    lp_ref[...] = total[40:72] * ((-2.0 * math.log(2.0)) * os_ref[0] / ls_ref[0])
    rhs = own_ref[64:104]
    off = eb - rhs
    off_ref[...] = off
    stacked = jnp.concatenate([rhs * rhs, rhs * off, off * off, jnp.zeros((8, LANES), f32)], axis=0)
    stat_ref[...] = jnp.sum(stacked.T, axis=0, keepdims=True)


def sums(lengthscale, outputscale, own, parts):
    return pl.pallas_call(
        sums_kernel,
        out_shape=[
            jax.ShapeDtypeStruct((PROBES, LANES), f32),
            jax.ShapeDtypeStruct((PROBES, LANES), f32),
            jax.ShapeDtypeStruct((40, LANES), f32),
            jax.ShapeDtypeStruct((1, LANES), f32),
        ],
        in_specs=[SMEM, SMEM, VMEM, VMEM],
        out_specs=[VMEM] * 4,
        name="sums",
    )(lengthscale, outputscale, own, parts)


def step_kernel(os_ref, noise_ref, own_ref, off_ref, stats_ref, sol_ref, res_ref, dir_ref):
    scale, noise = os_ref[0], noise_ref[0]
    row = jnp.sum(stats_ref[...], axis=0, keepdims=True)
    column = jnp.broadcast_to(row, (LANES, LANES)).T
    rr, rg, gg = column[0:40], column[40:80], column[80:120]
    rhs, off = own_ref[64:104], off_ref[...]
    curv = (scale + noise) * rr + scale * rg
    share = scale / curv
    sol = (rr / curv) * rhs
    res = share * (rg * rhs - rr * off)
    direction = res + (share * share * (rr * gg - rg * rg)) * rhs
    for ref, value in ((sol_ref, sol), (res_ref, res), (dir_ref, direction)):
        ref[0:1] = value[32:33]
        ref[1:33] = value[0:32]


def step(outputscale, noise, own, off, stats):
    return pl.pallas_call(
        step_kernel,
        out_shape=[jax.ShapeDtypeStruct((PROBES + 1, LANES), f32)] * 3,
        in_specs=[SMEM, SMEM, VMEM, VMEM, VMEM],
        out_specs=[VMEM] * 3,
        name="step",
    )(outputscale, noise, own, off, stats)


def spread(x, axes, count):
    return lax.all_to_all(jnp.broadcast_to(x[None], (count, *x.shape)), axes, 0, 0, tiled=True)


def shards(points, targets, probes, lengthscale, outputscale, noise):
    own = jnp.concatenate([points, probes, targets[None, :], jnp.zeros((7, LANES), f32)], 0)
    xi = spread(points, I_GROUP, N_I)
    xa = spread(own, J_GROUP, N_J)
    xb = lax.ppermute(xa, "co", [(0, 1), (1, 0)])
    parts = lax.all_to_all(products(lengthscale, xi, xa, xb), I_GROUP, 0, 0, tiled=True)
    lp, sp, off, stat = sums(lengthscale, outputscale, own, parts)
    stats = spread(stat[0], AXES, 512)
    sol, res, direction = step(outputscale, noise, own, off, stats)
    return sol, res, direction, lp, sp


def solution(mesh):
    apart = Mesh(mesh.devices.reshape(SIZES), AXES)
    split = P(None, AXES)
    return jax.shard_map(
        shards,
        mesh=apart,
        in_specs=(split, P(AXES), split, P(), P(), P()),
        out_specs=(split,) * 5,
        check_vma=False,
    )
```

time: 685 us -> 147 us (0.21)
  blocking collectives: 268 us -> 36 us
  waiting for transfers between devices: 244 us -> 37.3 us
  matrix products: 126 us -> 0 us
  starting transfers between devices: 0.12 us -> 34.3 us
  Pallas kernels: 0 us -> 30.1 us
  local copies, waits for them, and re-layouts: 19.8 us -> 5.22 us
  between operations: 15.9 us -> 2.65 us
    reduce_scatter x2 -> x0, waiting for transfers between devices: 242 us -> none  [the longest x1 123 us: shards(): lax.psum_scatter(ed_part, 'col', scatter_dimension=1, tiled=True)]
    psum x2 -> x0, blocking collectives: 194 us -> none  [the longest x1 99.8 us: shards(): lax.psum((jnp.sum(rhs * rhs, axis=1), jnp.sum(rhs * kb, axis=1)), ('row',...]
    dot_general x48 -> x0, matrix products: 126 us -> none  [the longest x16 51.8 us: step(): lax.dot_general(x_block, row_x, (((0,), (0,)), ((), ())), precision=lax.P...]
    all_gather x2 -> x0, blocking collectives: 74.2 us -> none  [the longest x1 42.3 us: shards(): lax.all_gather(rhs, 'row', axis=1, tiled=True)]
    all_to_all x0 -> x3, waiting for transfers between devices: none -> 37.3 us  [the longest x2 24.2 us: spread(): lax.all_to_all(jnp.broadcast_to(x[None], (count, *x.shape)), axes, 0, 0,...]
    all_to_all x0 -> x1, blocking collectives: none -> 36 us  [spread(): lax.all_to_all(jnp.broadcast_to(x[None], (count, *x.shape)), axes, 0, 0,...]
    pallas_call x0 -> x3, Pallas kernels: none -> 30.1 us  [the longest x1 26.5 us: products(): pl.pallas_call(products_kernel, out_shape=jax.ShapeDtypeStruct((N_I, BACK...]
    all_to_all x0 -> x3, starting transfers between devices: none -> 29.7 us  [the longest x2 25.4 us: spread(): lax.all_to_all(jnp.broadcast_to(x[None], (count, *x.shape)), axes, 0, 0,...]
  transfers between devices with their start and end apart: 3 -> 4, of which waited for: 2 -> 3; matrix products, arithmetic and copies ran while one was open for 1% -> 0% of each run, Pallas kernels for 0% -> 0%
where the time goes in v1:
time: 147 us; the launch traced here: 146 us
  waiting for transfers between devices  37.3 us (25%)
  blocking collectives  36 us (24%)
  starting transfers between devices  34.3 us (23%)
  Pallas kernels  30.1 us (20%)
  local copies, waits for them, and re-layouts  5.22 us (4%)
  between operations  2.65 us (2%)
    all_to_all x1, blocking collectives, spread(): lax.all_to_all(jnp.broadcast_to(x[None], (count, *x.shape)), axes, 0, 0,...  36 us
    pallas_call x1, Pallas kernels, products(): pl.pallas_call(products_kernel, out_shape=jax.ShapeDtypeStruct((N_I, BACK...  26.5 us
    all_to_all x2, starting transfers between devices, spread(): lax.all_to_all(jnp.broadcast_to(x[None], (count, *x.shape)), axes, 0, 0,...  25.4 us
    all_to_all x2, waiting for transfers between devices, spread(): lax.all_to_all(jnp.broadcast_to(x[None], (count, *x.shape)), axes, 0, 0,...  24.2 us
    all_to_all x1, waiting for transfers between devices, shards(): lax.all_to_all(products(lengthscale, xi, xa, xb), I_GROUP, 0, 0, tiled=True)  13.2 us
    ppermute x1, starting transfers between devices, shards(): xb = lax.ppermute(xa, 'co', [(0, 1), (1, 0)])  4.63 us
    all_to_all x1, starting transfers between devices, shards(): lax.all_to_all(products(lengthscale, xi, xa, xb), I_GROUP, 0, 0, tiled=True)  4.25 us
    unnamed x12, local copies, waits for them, and re-layouts  3.4 us
  transfers between devices with their start and end apart: 4, of which 3 were waited for; matrix products, arithmetic and copies ran while one was open for 0% of the time, Pallas kernels for 0%

profile of v1, /device:TPU:1, one launch (start us, length us, event | category | flops | bytes accessed | tf_op | source)
XLA Modules:
  0.0 146.4 jit_solution(15474987138870809464)
XLA Ops:
  0.6 0.1 pad.3.clone
  0.7 0.0 copy-start.4
  0.7 0.7 copy-done.4
  1.4 0.9 maximum_maximum_fusion.own_ref
  2.2 0.0 copy-start.2
  2.2 0.1 broadcast_in_dim.26
  2.3 0.6 copy-done.2
  2.9 0.0 copy-start.3
  2.9 36.0 %all_to_all.23.xa_ref = f32[16,104,128]{2,1,0:T(8,128)S(1)} all-to-all(f32[16,104,128]{2,1,0:T(8,128)S(1)} %broadcast_in_dim.26), channel_id=1, replica_groups=mesh['xh'=2,'z'=8,'y'=8,'xl'=2,'co'=2] {'xh','z'}, dimensions={0} | all-to-all | bytes 1703936 | tf_op jit(solution)/shard_map/all_to_all | solution.py:174
  38.8 0.0 copy-done.3
  38.8 0.8 broadcast_in_dim.12
  39.7 7.0 %all-to-all-start = ((f32[16,64,128]{2,1,0:T(8,128)}), f32[16,64,128]{2,1,0:T(8,128)S(1)}, u32[]{:S(2)}, u32[]{:S(2)}) async-start(f32[16,64,128]{2,1,0:T(8,128)} %broadcast_in_dim.12), calls=%async_computation | async-start | bytes 1048576 | tf_op jit(solution)/shard_map/all_to_all | solution.py:174
  46.6 4.6 %collective-permute-start = (f32[16,104,128]{2,1,0:T(8,128)S(1)}, f32[16,104,128]{2,1,0:T(8,128)S(1)}, u32[]{:S(2)}, u32[]{:S(2)}) collective-permute-start(f32[16,104,128]{2,1,0:T(8,128)S(1)} %all_to_all.23.xa_ref), channel_id=1, source_target_pairs={{0,1},{1,0},{2,3},{3,2},{4,5},{5,4},{6,7},{7,6},{8,9},{9,8},{10,11... | collective-permute-start | bytes 2555912 | tf_op jit(solution)/shard_map/ppermute | solution.py:181
  51.9 8.3 %all-to-all-done.xi_ref = f32[16,64,128]{2,1,0:T(8,128)S(1)} async-done(((f32[16,64,128]{2,1,0:T(8,128)}), f32[16,64,128]{2,1,0:T(8,128)S(1)}, u32[]{:S(2)}, u32[]{:S(2)}) %all-to-all-start) | async-done | bytes 524320 | tf_op jit(solution)/shard_map/all_to_all | solution.py:174
  60.2 0.0 collective-permute-done.xb_ref
  60.2 26.5 %products.1 = f32[16,72,128]{2,1,0:T(8,128)} custom-call(f32[1]{0:T(128)S(6)} %copy.11.ls_ref, f32[16,64,128]{2,1,0:T(8,128)S(1)} %all-to-all-done.xi_ref, f32[16,104,128]{2,1,0:T(8,128)S(1)} %all_to_all.23.xa_ref, f32[16,104,128]{2,1,0:T(8,128)S(1)} %collective-permute-done.xb_ref), custom_call_target="tpu_custom_call" | custom-call | flops 17179869184 | bytes 4194304 | tf_op jit(solution)/shard_map/products/pallas_call | solution.py:100
  86.8 4.3 %all-to-all-start.2 = ((f32[16,72,128]{2,1,0:T(8,128)}), f32[16,72,128]{2,1,0:T(8,128)S(1)}, u32[]{:S(2)}, u32[]{:S(2)}) async-start(f32[16,72,128]{2,1,0:T(8,128)} %products.1), calls=%async_computation.2 | async-start | bytes 1179648 | tf_op jit(solution)/shard_map/all_to_all | solution.py:182
  91.7 13.2 %all-to-all-done.2.part_ref = f32[16,72,128]{2,1,0:T(8,128)S(1)} async-done(((f32[16,72,128]{2,1,0:T(8,128)}), f32[16,72,128]{2,1,0:T(8,128)S(1)}, u32[]{:S(2)}, u32[]{:S(2)}) %all-to-all-start.2) | async-done | bytes 589856 | tf_op jit(solution)/shard_map/all_to_all | solution.py:182
  104.8 0.0 copy-start
  104.8 0.8 copy-done
  105.6 1.8 %sums.1 = (f32[32,128]{1,0:T(8,128)}, f32[32,128]{1,0:T(8,128)}, f32[40,128]{1,0:T(8,128)}, f32[1,128]{1,0:T(1,128)}) custom-call(f32[1]{0:T(128)S(6)} %copy.11.ls_ref, f32[1]{0:T(128)S(6)} %copy.12.os_ref, f32[104,128]{1,0:T(8,128)} %copy-done.2, f32[16,72,128]{2,1,0:T(8,128)} %copy-done), custom_call_target="tpu_custom_call" | custom-call | tf_op jit(solution)/shard_map/sums/pallas_call | solution.py:133
  107.4 0.0 copy-start.5
  107.4 0.7 copy-done.5
  108.1 0.8 broadcast_in_dim.27
  108.9 18.5 %all-to-all-start.3 = ((f32[512,1,128]{2,1,0:T(1,128)}), f32[512,1,128]{2,1,0:T(1,128)S(1)}, u32[]{:S(2)}, u32[]{:S(2)}) async-start(f32[512,1,128]{2,1,0:T(1,128)} %broadcast_in_dim.27), calls=%async_computation.3 | async-start | bytes 524288 | tf_op jit(solution)/shard_map/all_to_all | solution.py:174
  128.0 15.9 %all-to-all-done.3 = f32[512,1,128]{2,1,0:T(1,128)S(1)} async-done(((f32[512,1,128]{2,1,0:T(1,128)}), f32[512,1,128]{2,1,0:T(1,128)S(1)}, u32[]{:S(2)}, u32[]{:S(2)}) %all-to-all-start.3) | async-done | bytes 262176 | tf_op jit(solution)/shard_map/all_to_all | solution.py:174
  143.9 0.0 copy-start.1
  143.9 0.7 copy-done.1
  144.6 1.8 %step.1 = (f32[33,128]{1,0:T(8,128)}, f32[33,128]{1,0:T(8,128)}, f32[33,128]{1,0:T(8,128)}) custom-call(f32[1]{0:T(128)S(6)} %copy.12.os_ref, f32[1]{0:T(128)S(6)} %copy.13.noise_ref, f32[104,128]{1,0:T(8,128)} %copy-done.2, f32[40,128]{1,0:T(8,128)} %get-tuple-element.12.off_ref, f32[512,128]{1,0:T(8,128)} %bitcast.3), custom_call_target="tpu_custom_call" | custom-call | tf_op jit(solution)/shard_map/step/pallas_call | solution.py:164
  (1 shorter events, 0.0 us)
Async XLA Ops:
  0.7 0.7 copy-start.4
  2.2 0.6 copy-start.2
  2.9 36.0 %copy-start.3 = (f32[64,128]{1,0:T(8,128)S(1)}, f32[64,128]{1,0:T(8,128)}, u32[]{:S(2)}) copy-start(f32[64,128]{1,0:T(8,128)} %param.6) | copy-start | bytes 98308
  39.7 20.6 %all-to-all-start = ((f32[16,64,128]{2,1,0:T(8,128)}), f32[16,64,128]{2,1,0:T(8,128)S(1)}, u32[]{:S(2)}, u32[]{:S(2)}) async-start(f32[16,64,128]{2,1,0:T(8,128)} %broadcast_in_dim.12), calls=%async_computation | async-start | bytes 1048576 | tf_op jit(solution)/shard_map/all_to_all | solution.py:174
  46.6 13.6 %collective-permute-start = (f32[16,104,128]{2,1,0:T(8,128)S(1)}, f32[16,104,128]{2,1,0:T(8,128)S(1)}, u32[]{:S(2)}, u32[]{:S(2)}) collective-permute-start(f32[16,104,128]{2,1,0:T(8,128)S(1)} %all_to_all.23.xa_ref), channel_id=1, source_target_pairs={{0,1},{1,0},{2,3},{3,2},{4,5},{5,4},{6,7},{7,6},{8,9},{9,8},{10,11... | collective-permute-start | bytes 2555912 | tf_op jit(solution)/shard_map/ppermute | solution.py:181
  86.8 18.1 %all-to-all-start.2 = ((f32[16,72,128]{2,1,0:T(8,128)}), f32[16,72,128]{2,1,0:T(8,128)S(1)}, u32[]{:S(2)}, u32[]{:S(2)}) async-start(f32[16,72,128]{2,1,0:T(8,128)} %products.1), calls=%async_computation.2 | async-start | bytes 1179648 | tf_op jit(solution)/shard_map/all_to_all | solution.py:182
  104.8 0.8 copy-start
  107.4 0.7 copy-start.5
  108.9 35.0 %all-to-all-start.3 = ((f32[512,1,128]{2,1,0:T(1,128)}), f32[512,1,128]{2,1,0:T(1,128)S(1)}, u32[]{:S(2)}, u32[]{:S(2)}) async-start(f32[512,1,128]{2,1,0:T(1,128)} %broadcast_in_dim.27), calls=%async_computation.3 | async-start | bytes 524288 | tf_op jit(solution)/shard_map/all_to_all | solution.py:174
  143.9 0.7 copy-start.1

commit v2 on v1

v2 whole, which is shorter than its diff:
```python
import math

import jax
import jax.numpy as jnp
from jax import lax
from jax.experimental import pallas as pl
from jax.experimental.pallas import tpu as pltpu
from jax.sharding import Mesh, PartitionSpec as P

AXES = ("xh", "zh", "zm", "za", "yb", "ya", "xl", "co")
SIZES = (2, 2, 2, 2, 4, 2, 2, 2)
I_GROUP = ("ya", "za", "xh", "xl")
J_GROUP = ("yb", "zh", "zm")
SUM_FIRST = ("yb", "ya", "co")
SUM_LAST = ("xh", "xl", "zh", "zm", "za")
N_I = 16
N_J = 16
N_FIRST = 16
N_LAST = 32
LANES = 128
F = 64
PROBES = 32
RHS = 40
SENT = F + RHS
BACK = RHS + PROBES
HALF = 48
BI = 256
UNROLL = 8
PRODUCTS_MIB = 32
f32, bf16 = jnp.float32, jnp.bfloat16
LOG2E = math.log2(math.e)
VMEM = pl.BlockSpec(memory_space=pltpu.VMEM)
SMEM = pl.BlockSpec(memory_space=pltpu.SMEM)


def small(mib=8):
    return pltpu.CompilerParams(vmem_limit_bytes=mib << 20)


def shaped(*shape, dtype=f32):
    return jax.ShapeDtypeStruct(shape, dtype)


def halves(x):
    hi = x.astype(bf16)
    return hi, (x - hi.astype(f32)).astype(bf16)


def tile(t, size=LANES):
    return pl.ds(pl.multiple_of(t * size, size), size)


def rate(ls_ref):
    ell = ls_ref[0]
    return (0.5 * LOG2E) / (ell * ell)


def pack_kernel(points_ref, probes_ref, targets_ref, to_j_ref, rhs_ref):
    x = points_ref[...]
    rhs_ref[0:32] = probes_ref[...]
    rhs_ref[32:40] = jnp.concatenate([targets_ref[...], jnp.zeros((7, LANES), f32)], axis=0)
    rhs = rhs_ref[...]
    for t in range(N_J):
        to_j_ref[t, 0:F] = x
        to_j_ref[t, F:SENT] = rhs


def pack(points, probes, targets):
    return pl.pallas_call(
        pack_kernel,
        out_shape=[shaped(N_J, SENT, LANES), shaped(RHS, LANES)],
        in_specs=[VMEM] * 3,
        out_specs=[VMEM] * 2,
        compiler_params=small(60),
        cost_estimate=pl.CostEstimate(flops=0, bytes_accessed=2 << 20, transcendentals=0),
        name="pack",
    )(points, probes, targets[None, :])


def products_kernel(ls_ref, me_ref, *refs):
    xi_refs, xj_ref, acc_refs, (out_ref, left, sq_i, right, sq_j, rhs) = refs[:5], refs[5], refs[6:-6], refs[-6:]
    c = rate(ls_ref)

    def prepare_j(t, unused):
        hi, lo = halves(xj_ref[t, 0:F])
        x = hi.astype(f32) + lo.astype(f32)
        at = tile(t)
        turned = jnp.concatenate([hi.astype(f32), lo.astype(f32)], axis=0).T.astype(bf16)
        right[at, 0:64] = turned[:, 0:64]
        right[at, 64:128] = turned[:, 0:64]
        right[at, 128:192] = turned[:, 64:128]
        right[at, 192:256] = turned[:, 64:128]
        sq = jnp.broadcast_to(-c * jnp.sum(x * x, axis=0, keepdims=True), (LANES, LANES))
        sq_j[at, :] = sq.T
        b = jnp.concatenate([xj_ref[t, F:SENT], jnp.zeros((HALF - RHS, LANES), f32)], axis=0)
        bh, bl = halves(b)
        rhs[0:HALF, at] = bh
        rhs[HALF : 2 * HALF, at] = bl
        return unused

    lax.fori_loop(0, N_J, prepare_j, 0, unroll=True)

    def prepare_i(points, place):
        hi, lo = halves(points)
        x = hi.astype(f32) + lo.astype(f32)
        yh, yl = halves((2.0 * c) * x)
        at = tile(jnp.bitwise_xor(place, me_ref[0]))
        left[0:64, at] = yh
        left[64:128, at] = yl
        left[128:192, at] = yh
        left[192:256, at] = yl
        sq_i[:, at] = jnp.broadcast_to(-c * jnp.sum(x * x, axis=0, keepdims=True), (8, LANES))

    prepare_i(xi_refs[0][...], 0)
    for s in range(4):
        for t in range(1 << s):
            prepare_i(xi_refs[1 + s][t], (1 << s) + t)

    def block(ib, unused):
        at = tile(ib, BI)
        dots = jnp.dot(right[...], left[:, at], preferred_element_type=f32)
        sq = jnp.concatenate([sq_j[...]] * (BI // LANES), axis=1)
        power = jnp.minimum(dots + sq_i[0:1, at] + sq, 0.0)
        kern = jnp.exp2(power)
        kh, kl = halves(kern)
        dh, dl = halves(kern * power)
        b, d, bl, dl = (jnp.dot(rhs[...], m, preferred_element_type=f32) for m in (kh, dh, kl, dl))
        b, d = b + bl, d + dl
        b = b[0:RHS] + b[HALF : HALF + RHS]
        d = d[0:PROBES] + d[HALF : HALF + PROBES]
        both = jnp.concatenate([b, d], axis=0)
        for p in range(BI // LANES):
            t = ib * (BI // LANES) + p
            part = both[:, p * LANES : (p + 1) * LANES]
            out_ref[t] = acc_refs[0][t] + part if acc_refs else part
        return unused

    lax.fori_loop(0, N_I * LANES // BI, block, 0, unroll=UNROLL)


def products(lengthscale, me, xi, xj, *acc):
    rows, cols = N_I * LANES, N_J * LANES
    return pl.pallas_call(
        products_kernel,
        out_shape=shaped(N_I, BACK, LANES),
        in_specs=[SMEM] * 2 + [VMEM] * (6 + len(acc)),
        out_specs=VMEM,
        scratch_shapes=[
            pltpu.VMEM((256, rows), bf16),
            pltpu.VMEM((8, rows), f32),
            pltpu.VMEM((cols, 256), bf16),
            pltpu.VMEM((cols, LANES), f32),
            pltpu.VMEM((2 * HALF, cols), bf16),
        ],
        compiler_params=small(PRODUCTS_MIB),
        cost_estimate=pl.CostEstimate(flops=2 * rows * cols * 1280, bytes_accessed=2 << 20, transcendentals=rows * cols),
        name="products",
    )(lengthscale, me, *xi, xj, *acc)


def sums_kernel(ls_ref, os_ref, rhs_ref, part_ref, lp_ref, sp_ref, off_ref, stat_ref):
    total = part_ref[0]
    for s in range(1, N_I):
        total = total + part_ref[s]
    eb = total[0:RHS]
    sp_ref[...] = eb[0:PROBES]
    lp_ref[...] = total[RHS:BACK] * ((-2.0 * math.log(2.0)) * os_ref[0] / ls_ref[0])
    rhs = rhs_ref[...]
    off = eb - rhs
    off_ref[...] = off
    stacked = jnp.concatenate([rhs * rhs, rhs * off, off * off, jnp.zeros((8, LANES), f32)], axis=0)
    stat_ref[...] = jnp.broadcast_to(jnp.sum(stacked.T, axis=0, keepdims=True), (N_FIRST, LANES))


def sums(lengthscale, outputscale, rhs, parts):
    return pl.pallas_call(
        sums_kernel,
        out_shape=[shaped(PROBES, LANES), shaped(PROBES, LANES), shaped(RHS, LANES), shaped(N_FIRST, LANES)],
        in_specs=[SMEM, SMEM, VMEM, VMEM],
        out_specs=[VMEM] * 4,
        compiler_params=small(),
        name="sums",
    )(lengthscale, outputscale, rhs, parts)


def again_kernel(stats_ref, out_ref):
    out_ref[...] = jnp.broadcast_to(jnp.sum(stats_ref[...], axis=0, keepdims=True), (N_LAST, LANES))


def again(stats):
    return pl.pallas_call(
        again_kernel, out_shape=shaped(N_LAST, LANES), in_specs=[VMEM], out_specs=VMEM, compiler_params=small(), name="again"
    )(stats)


def step_kernel(os_ref, noise_ref, rhs_ref, off_ref, stats_ref, sol_ref, res_ref, dir_ref):
    scale, noise = os_ref[0], noise_ref[0]
    row = jnp.sum(stats_ref[...], axis=0, keepdims=True)
    column = jnp.broadcast_to(row, (LANES, LANES)).T
    rr, rg, gg = column[0:RHS], column[RHS : 2 * RHS], column[2 * RHS : 3 * RHS]
    rhs, off = rhs_ref[...], off_ref[...]
    curv = (scale + noise) * rr + scale * rg
    share = scale / curv
    sol = (rr / curv) * rhs
    res = share * (rg * rhs - rr * off)
    direction = res + (share * share * (rr * gg - rg * rg)) * rhs
    for ref, value in ((sol_ref, sol), (res_ref, res), (dir_ref, direction)):
        ref[0:1] = value[32:33]
        ref[1:33] = value[0:32]


def step(outputscale, noise, rhs, off, stats):
    return pl.pallas_call(
        step_kernel,
        out_shape=[shaped(PROBES + 1, LANES)] * 3,
        in_specs=[SMEM, SMEM, VMEM, VMEM, VMEM],
        out_specs=[VMEM] * 3,
        compiler_params=small(),
        name="step",
    )(outputscale, noise, rhs, off, stats)


def exchange(x, axes):
    return lax.all_to_all(x, axes, 0, 0, tiled=True)


def swap(x, axis):
    return lax.ppermute(x, axis, [(0, 1), (1, 0)])


def shards(points, targets, probes, lengthscale, outputscale, noise):
    to_j, rhs = pack(points, probes, targets)
    xa = exchange(to_j, J_GROUP)
    pieces, held = [points], points[None]
    for axis in reversed(I_GROUP):
        pieces.append(swap(held, axis))
        held = jnp.concatenate([held, pieces[-1]], axis=0)
    xb = swap(xa, "co")
    me = lax.axis_index(I_GROUP).reshape(1)
    half = products(lengthscale, me, pieces, xa)
    parts = exchange(products(lengthscale, me, pieces, xb, half), I_GROUP)
    lp, sp, off, stat = sums(lengthscale, outputscale, rhs, parts)
    stats = exchange(again(exchange(stat, SUM_FIRST)), SUM_LAST)
    sol, res, direction = step(outputscale, noise, rhs, off, stats)
    return sol, res, direction, lp, sp


def solution(mesh):
    apart = Mesh(mesh.devices.reshape(SIZES), AXES)
    split = P(None, AXES)
    return jax.shard_map(
        shards,
        mesh=apart,
        in_specs=(split, P(AXES), split, P(), P(), P()),
        out_specs=(split,) * 5,
        check_vma=False,
    )
```

time: 147 us -> 124 us (0.84)
  blocking collectives: 36 us -> 15.3 us
  starting transfers between devices: 34.3 us -> 50 us
  waiting for transfers between devices: 37.3 us -> 30.4 us
  local copies, waits for them, and re-layouts: 5.22 us -> 0.01 us
  Pallas kernels: 30.1 us -> 25.1 us
    all_to_all x1, blocking collectives: 36 us -> 15.3 us  [exchange(): return lax.all_to_all(x, axes, 0, 0, tiled=True)]
    all_to_all x3, waiting for transfers between devices: 37.3 us -> 17.1 us  [exchange(): return lax.all_to_all(x, axes, 0, 0, tiled=True)]
    ppermute x1 -> x5, starting transfers between devices: 4.63 us -> 19.1 us  [swap(): return lax.ppermute(x, axis, [(0, 1), (1, 0)])]
    ppermute x1 -> x5, waiting for transfers between devices: 0.01 us -> 13.3 us  [swap(): return lax.ppermute(x, axis, [(0, 1), (1, 0)])]
    pallas_call x3 -> x6, Pallas kernels: 30.1 us -> 25.1 us  [the longest x2 21.3 us: products(): pl.pallas_call(products_kernel, out_shape=shaped(N_I, BACK, LANES), in_sp...]
    unnamed x12 -> x4, local copies, waits for them, and re-layouts: 3.4 us -> 0.01 us
    broadcast_in_dim x4 -> x0, local copies, waits for them, and re-layouts: 1.74 us -> none  [the longest x3 1.74 us: spread(): jnp.broadcast_to(x[None], (count, *x.shape))]
  transfers between devices with their start and end apart: 4 -> 8, of which waited for: 3 -> 5; matrix products, arithmetic and copies ran while one was open for 0% -> 0% of each run, Pallas kernels for 0% -> 8%
where the time goes in v2:
time: 124 us; the launch traced here: 123 us
  starting transfers between devices  50 us (40%)
  waiting for transfers between devices  30.4 us (25%)
  Pallas kernels  25.1 us (20%)
  blocking collectives  15.3 us (12%)
  between operations  2.71 us (2%)
    all_to_all x3, starting transfers between devices, exchange(): return lax.all_to_all(x, axes, 0, 0, tiled=True)  30.9 us
    pallas_call x2, Pallas kernels, products(): pl.pallas_call(products_kernel, out_shape=shaped(N_I, BACK, LANES), in_sp...  21.3 us
    ppermute x5, starting transfers between devices, swap(): return lax.ppermute(x, axis, [(0, 1), (1, 0)])  19.1 us
    all_to_all x3, waiting for transfers between devices, exchange(): return lax.all_to_all(x, axes, 0, 0, tiled=True)  17.1 us
    all_to_all x1, blocking collectives, exchange(): return lax.all_to_all(x, axes, 0, 0, tiled=True)  15.3 us
    ppermute x5, waiting for transfers between devices, swap(): return lax.ppermute(x, axis, [(0, 1), (1, 0)])  13.3 us
  transfers between devices with their start and end apart: 8, of which 5 were waited for; matrix products, arithmetic and copies ran while one was open for 0% of the time, Pallas kernels for 8%

profile of v2, /device:TPU:1, one launch (start us, length us, event | category | flops | bytes accessed | tf_op | source)
XLA Modules:
  0.0 123.4 jit_solution(936764947586874812)
XLA Ops:
  0.6 1.7 %pack.1 = (f32[16,104,128]{2,1,0:T(8,128)}, f32[40,128]{1,0:T(8,128)}) custom-call(f32[64,128]{1,0:T(8,128)} %refs_0_.3, f32[32,128]{1,0:T(8,128)} %probes_ref.1, f32[1,128]{1,0:T(1,128)} %bitcast.18), custom_call_target="tpu_custom_call" | custom-call | bytes 2097152 | tf_op jit(solution)/shard_map/pack/pallas_call | solution.py:69
  2.4 0.0 copy-start
  2.4 16.4 %all-to-all-start = ((f32[16,104,128]{2,1,0:T(8,128)}), f32[16,104,128]{2,1,0:T(8,128)S(1)}, u32[]{:S(2)}, u32[]{:S(2)}) async-start(f32[16,104,128]{2,1,0:T(8,128)} %get-tuple-element.15), calls=%async_computation | async-start | bytes 1703936 | tf_op jit(solution)/shard_map/all_to_all | solution.py:224
  18.7 0.0 copy-done
  18.7 3.1 %collective-permute-start = (f32[1,64,128]{2,1,0:T(8,128)S(1)}, f32[1,64,128]{2,1,0:T(8,128)S(1)}, u32[]{:S(2)}, u32[]{:S(2)}) collective-permute-start(f32[1,64,128]{2,1,0:T(8,128)S(1)} %bitcast.11), channel_id=1, source_target_pairs={{0,2},{2,0},{1,3},{3,1},{4,6},{6,4},{5,7},{7,5},{8,10},{10,8},{9,1... | collective-permute-start | bytes 98312 | tf_op jit(solution)/shard_map/ppermute | solution.py:228
  21.9 1.5 %collective-permute-done.refs_1_ = f32[1,64,128]{2,1,0:T(8,128)S(1)} collective-permute-done((f32[1,64,128]{2,1,0:T(8,128)S(1)}, f32[1,64,128]{2,1,0:T(8,128)S(1)}, u32[]{:S(2)}, u32[]{:S(2)}) %collective-permute-start) | collective-permute-done | bytes 32800 | tf_op jit(solution)/shard_map/ppermute | solution.py:228
  23.4 4.6 %collective-permute-start.1 = (f32[2,64,128]{2,1,0:T(8,128)S(1)}, f32[2,64,128]{2,1,0:T(8,128)S(1)}, u32[]{:S(2)}, u32[]{:S(2)}) collective-permute-start(f32[2,64,128]{2,1,0:T(8,128)S(1)} %pad_maximum_fusion.2), channel_id=1, source_target_pairs={{0,256},{256,0},{1,257},{257,1},{2,258},{258,2},{3,259},{259,3},{4... | collective-permute-start | bytes 196616 | tf_op jit(solution)/shard_map/ppermute | solution.py:228
  28.1 1.9 %collective-permute-done.1.refs_2_ = f32[2,64,128]{2,1,0:T(8,128)S(1)} collective-permute-done((f32[2,64,128]{2,1,0:T(8,128)S(1)}, f32[2,64,128]{2,1,0:T(8,128)S(1)}, u32[]{:S(2)}, u32[]{:S(2)}) %collective-permute-start.1) | collective-permute-done | bytes 65568 | tf_op jit(solution)/shard_map/ppermute | solution.py:228
  29.9 3.1 %collective-permute-start.2 = (f32[4,64,128]{2,1,0:T(8,128)S(1)}, f32[4,64,128]{2,1,0:T(8,128)S(1)}, u32[]{:S(2)}, u32[]{:S(2)}) collective-permute-start(f32[4,64,128]{2,1,0:T(8,128)S(1)} %pad_maximum_fusion.1), channel_id=1, source_target_pairs={{0,32},{32,0},{1,33},{33,1},{2,34},{34,2},{3,35},{35,3},{4,36},{36... | collective-permute-start | bytes 393224 | tf_op jit(solution)/shard_map/ppermute | solution.py:228
  33.0 9.9 %collective-permute-done.2.refs_3_ = f32[4,64,128]{2,1,0:T(8,128)S(1)} collective-permute-done((f32[4,64,128]{2,1,0:T(8,128)S(1)}, f32[4,64,128]{2,1,0:T(8,128)S(1)}, u32[]{:S(2)}, u32[]{:S(2)}) %collective-permute-start.2) | collective-permute-done | bytes 131104 | tf_op jit(solution)/shard_map/ppermute | solution.py:228
  43.0 2.5 %collective-permute-start.3 = (f32[8,64,128]{2,1,0:T(8,128)S(1)}, f32[8,64,128]{2,1,0:T(8,128)S(1)}, u32[]{:S(2)}, u32[]{:S(2)}) collective-permute-start(f32[8,64,128]{2,1,0:T(8,128)S(1)} %pad_maximum_fusion), channel_id=1, source_target_pairs={{0,4},{4,0},{1,5},{5,1},{2,6},{6,2},{3,7},{7,3},{8,12},{12,8},{9,1... | collective-permute-start | bytes 786440 | tf_op jit(solution)/shard_map/ppermute | solution.py:228
  46.2 0.0 all-to-all-done.refs_5_
  46.2 5.7 %collective-permute-start.4 = (f32[16,104,128]{2,1,0:T(8,128)S(1)}, f32[16,104,128]{2,1,0:T(8,128)S(1)}, u32[]{:S(2)}, u32[]{:S(2)}) collective-permute-start(f32[16,104,128]{2,1,0:T(8,128)S(1)} %all-to-all-done.refs_5_), channel_id=1, source_target_pairs={{0,1},{1,0},{2,3},{3,2},{4,5},{5,4},{6,7},{7,6},{8,9},{9,8},{10,11... | collective-permute-start | bytes 2555912 | tf_op jit(solution)/shard_map/ppermute | solution.py:228
  51.9 0.0 collective-permute-done.3.refs_4_
  51.9 10.1 %products.2.refs_6_ = f32[16,72,128]{2,1,0:T(8,128)S(1)} custom-call(f32[1]{0:T(128)S(6)} %copy.13.ls_ref, s32[1]{0:T(128)} %bitcast.1.me_ref, f32[64,128]{1,0:T(8,128)S(1)} %copy-done, f32[1,64,128]{2,1,0:T(8,128)S(1)} %collective-permute-done.refs_1_, f32[2,64,128]{2,1,0:T(8,128)S(1)} %collective-permute-done.1.refs_2_, ...), custom_call_target="tpu_custom_call" | custom-call | flops 10737418240 | bytes 2097152 | tf_op jit(solution)/shard_map/products/pallas_call | solution.py:143
  62.0 0.0 collective-permute-done.4.refs_5_
  62.0 11.2 %products.3 = f32[16,72,128]{2,1,0:T(8,128)} custom-call(f32[1]{0:T(128)S(6)} %copy.13.ls_ref, s32[1]{0:T(128)} %bitcast.1.me_ref, f32[64,128]{1,0:T(8,128)S(1)} %copy-done, f32[1,64,128]{2,1,0:T(8,128)S(1)} %collective-permute-done.refs_1_, f32[2,64,128]{2,1,0:T(8,128)S(1)} %collective-permute-done.1.refs_2_, ...), custom_call_target="tpu_custom_call" | custom-call | flops 10737418240 | bytes 2097152 | tf_op jit(solution)/shard_map/products/pallas_call | solution.py:143
  73.3 0.0 copy-start.1
  73.3 7.4 %all-to-all-start.1 = ((f32[16,72,128]{2,1,0:T(8,128)}), f32[16,72,128]{2,1,0:T(8,128)S(1)}, u32[]{:S(2)}, u32[]{:S(2)}) async-start(f32[16,72,128]{2,1,0:T(8,128)} %products.3), calls=%async_computation.1 | async-start | bytes 1179648 | tf_op jit(solution)/shard_map/all_to_all | solution.py:224
  81.3 9.1 %all-to-all-done.1.part_ref = f32[16,72,128]{2,1,0:T(8,128)S(1)} async-done(((f32[16,72,128]{2,1,0:T(8,128)}), f32[16,72,128]{2,1,0:T(8,128)S(1)}, u32[]{:S(2)}, u32[]{:S(2)}) %all-to-all-start.1) | async-done | bytes 589856 | tf_op jit(solution)/shard_map/all_to_all | solution.py:224
  90.5 0.0 copy-done.1
  90.5 0.7 sums.1
  91.1 15.3 %all_to_all.32 = f32[16,1,128]{2,1,0:T(1,128)S(1)} all-to-all(f32[16,1,128]{2,1,0:T(1,128)S(1)} %bitcast.17), channel_id=1, replica_groups=mesh['xh'=2,'zh'=2,'zm'=2,'za'=2,'yb'=4,'ya'=2,'xl'=2,'co'=2] {'yb','ya'..., dimensions={0} | all-to-all | bytes 16384 | tf_op jit(solution)/shard_map/all_to_all | solution.py:224
  106.4 0.6 again.1
  107.0 7.1 %all-to-all-start.3 = ((f32[32,1,128]{2,1,0:T(1,128)}), f32[32,1,128]{2,1,0:T(1,128)S(1)}, u32[]{:S(2)}, u32[]{:S(2)}) async-start(f32[32,1,128]{2,1,0:T(1,128)} %bitcast.7), calls=%async_computation.3 | async-start | bytes 32768 | tf_op jit(solution)/shard_map/all_to_all | solution.py:224
  114.8 7.9 %all-to-all-done.3 = f32[32,1,128]{2,1,0:T(1,128)S(1)} async-done(((f32[32,1,128]{2,1,0:T(1,128)}), f32[32,1,128]{2,1,0:T(1,128)S(1)}, u32[]{:S(2)}, u32[]{:S(2)}) %all-to-all-start.3) | async-done | bytes 16416 | tf_op jit(solution)/shard_map/all_to_all | solution.py:224
  122.7 0.7 step.1
  (3 shorter events, 0.0 us)
Async XLA Ops:
  2.4 16.4 %copy-start = (f32[64,128]{1,0:T(8,128)S(1)}, f32[64,128]{1,0:T(8,128)}, u32[]{:S(2)}) copy-start(f32[64,128]{1,0:T(8,128)} %refs_0_.3) | copy-start | bytes 98308
  2.4 43.8 %all-to-all-start = ((f32[16,104,128]{2,1,0:T(8,128)}), f32[16,104,128]{2,1,0:T(8,128)S(1)}, u32[]{:S(2)}, u32[]{:S(2)}) async-start(f32[16,104,128]{2,1,0:T(8,128)} %get-tuple-element.15), calls=%async_computation | async-start | bytes 1703936 | tf_op jit(solution)/shard_map/all_to_all | solution.py:224
  18.7 4.7 %collective-permute-start = (f32[1,64,128]{2,1,0:T(8,128)S(1)}, f32[1,64,128]{2,1,0:T(8,128)S(1)}, u32[]{:S(2)}, u32[]{:S(2)}) collective-permute-start(f32[1,64,128]{2,1,0:T(8,128)S(1)} %bitcast.11), channel_id=1, source_target_pairs={{0,2},{2,0},{1,3},{3,1},{4,6},{6,4},{5,7},{7,5},{8,10},{10,8},{9,1... | collective-permute-start | bytes 98312 | tf_op jit(solution)/shard_map/ppermute | solution.py:228
  23.4 6.5 %collective-permute-start.1 = (f32[2,64,128]{2,1,0:T(8,128)S(1)}, f32[2,64,128]{2,1,0:T(8,128)S(1)}, u32[]{:S(2)}, u32[]{:S(2)}) collective-permute-start(f32[2,64,128]{2,1,0:T(8,128)S(1)} %pad_maximum_fusion.2), channel_id=1, source_target_pairs={{0,256},{256,0},{1,257},{257,1},{2,258},{258,2},{3,259},{259,3},{4... | collective-permute-start | bytes 196616 | tf_op jit(solution)/shard_map/ppermute | solution.py:228
  29.9 13.0 %collective-permute-start.2 = (f32[4,64,128]{2,1,0:T(8,128)S(1)}, f32[4,64,128]{2,1,0:T(8,128)S(1)}, u32[]{:S(2)}, u32[]{:S(2)}) collective-permute-start(f32[4,64,128]{2,1,0:T(8,128)S(1)} %pad_maximum_fusion.1), channel_id=1, source_target_pairs={{0,32},{32,0},{1,33},{33,1},{2,34},{34,2},{3,35},{35,3},{4,36},{36... | collective-permute-start | bytes 393224 | tf_op jit(solution)/shard_map/ppermute | solution.py:228
  43.0 9.0 %collective-permute-start.3 = (f32[8,64,128]{2,1,0:T(8,128)S(1)}, f32[8,64,128]{2,1,0:T(8,128)S(1)}, u32[]{:S(2)}, u32[]{:S(2)}) collective-permute-start(f32[8,64,128]{2,1,0:T(8,128)S(1)} %pad_maximum_fusion), channel_id=1, source_target_pairs={{0,4},{4,0},{1,5},{5,1},{2,6},{6,2},{3,7},{7,3},{8,12},{12,8},{9,1... | collective-permute-start | bytes 786440 | tf_op jit(solution)/shard_map/ppermute | solution.py:228
  46.2 15.9 %collective-permute-start.4 = (f32[16,104,128]{2,1,0:T(8,128)S(1)}, f32[16,104,128]{2,1,0:T(8,128)S(1)}, u32[]{:S(2)}, u32[]{:S(2)}) collective-permute-start(f32[16,104,128]{2,1,0:T(8,128)S(1)} %all-to-all-done.refs_5_), channel_id=1, source_target_pairs={{0,1},{1,0},{2,3},{3,2},{4,5},{5,4},{6,7},{7,6},{8,9},{9,8},{10,11... | collective-permute-start | bytes 2555912 | tf_op jit(solution)/shard_map/ppermute | solution.py:228
  73.3 17.2 %copy-start.1 = (f32[40,128]{1,0:T(8,128)S(1)}, f32[40,128]{1,0:T(8,128)}, u32[]{:S(2)}) copy-start(f32[40,128]{1,0:T(8,128)} %get-tuple-element.14.rhs_ref) | copy-start | bytes 61444
  73.3 17.2 %all-to-all-start.1 = ((f32[16,72,128]{2,1,0:T(8,128)}), f32[16,72,128]{2,1,0:T(8,128)S(1)}, u32[]{:S(2)}, u32[]{:S(2)}) async-start(f32[16,72,128]{2,1,0:T(8,128)} %products.3), calls=%async_computation.1 | async-start | bytes 1179648 | tf_op jit(solution)/shard_map/all_to_all | solution.py:224
  107.0 15.7 %all-to-all-start.3 = ((f32[32,1,128]{2,1,0:T(1,128)}), f32[32,1,128]{2,1,0:T(1,128)S(1)}, u32[]{:S(2)}, u32[]{:S(2)}) async-start(f32[32,1,128]{2,1,0:T(1,128)} %bitcast.7), calls=%async_computation.3 | async-start | bytes 32768 | tf_op jit(solution)/shard_map/all_to_all | solution.py:224

commit v3 on v2

v3 whole, which is shorter than its diff:
```python
import math

import jax
import jax.numpy as jnp
from jax import lax
from jax.experimental import pallas as pl
from jax.experimental.pallas import tpu as pltpu
from jax.sharding import Mesh, PartitionSpec as P

AXES = ("xh", "zh", "zm", "za", "yb", "ya", "xl", "co")
SIZES = (2, 2, 2, 2, 4, 2, 2, 2)
I_GROUP = ("za", "ya", "xh", "xl")
J_GROUP = ("yb", "zh", "zm")
SUM_FIRST = ("yb", "ya", "co")
SUM_LAST = ("xh", "xl", "zh", "zm", "za")
N_I = 16
N_J = 16
N_FIRST = 16
N_LAST = 32
LANES = 128
F = 64
PROBES = 32
RHS = 40
SENT = F + RHS
BACK = RHS + PROBES
HALF = 48
BI = 256
PRODUCTS_MIB = 32
f32, bf16 = jnp.float32, jnp.bfloat16
LOG2E = math.log2(math.e)
VMEM = pl.BlockSpec(memory_space=pltpu.VMEM)
SMEM = pl.BlockSpec(memory_space=pltpu.SMEM)


def small(mib=8):
    return pltpu.CompilerParams(vmem_limit_bytes=mib << 20)


def shaped(*shape, dtype=f32):
    return jax.ShapeDtypeStruct(shape, dtype)


def halves(x):
    hi = x.astype(bf16)
    return hi, (x - hi.astype(f32)).astype(bf16)


def tile(t, size=LANES):
    return pl.ds(pl.multiple_of(t * size, size), size)


def pack_kernel(points_ref, probes_ref, targets_ref, to_j_ref, rhs_ref):
    x = points_ref[...]
    rhs_ref[0:32] = probes_ref[...]
    rhs_ref[32:40] = jnp.concatenate([targets_ref[...], jnp.zeros((7, LANES), f32)], axis=0)
    rhs = rhs_ref[...]
    for t in range(N_J):
        to_j_ref[t, 0:F] = x
        to_j_ref[t, F:SENT] = rhs


def pack(points, probes, targets):
    return pl.pallas_call(
        pack_kernel,
        out_shape=[shaped(N_J, SENT, LANES), shaped(RHS, LANES)],
        in_specs=[VMEM] * 3,
        out_specs=[VMEM] * 2,
        compiler_params=small(60),
        cost_estimate=pl.CostEstimate(flops=0, bytes_accessed=2 << 20, transcendentals=0),
        name="pack",
    )(points, probes, targets[None, :])


def prepare_j(c, xj_ref, right, sq_j, rhs):
    for t in range(N_J):
        hi, lo = halves(xj_ref[t, 0:F])
        x = hi.astype(f32) + lo.astype(f32)
        at = slice(t * LANES, (t + 1) * LANES)
        turned = jnp.concatenate([hi.astype(f32), lo.astype(f32)], axis=0).T.astype(bf16)
        right[at, 0:64] = turned[:, 0:64]
        right[at, 64:128] = turned[:, 0:64]
        right[at, 128:192] = turned[:, 64:128]
        right[at, 192:256] = turned[:, 64:128]
        sq = jnp.broadcast_to(-c * jnp.sum(x * x, axis=0, keepdims=True), (LANES, LANES))
        sq_j[at, :] = sq.T
        b = jnp.concatenate([xj_ref[t, F:SENT], jnp.zeros((HALF - RHS, LANES), f32)], axis=0)
        bh, bl = halves(b)
        rhs[0:HALF, at] = bh
        rhs[HALF : 2 * HALF, at] = bl


def blocks(left, sq_i, right, sq_j, rhs, acc_ref, out_ref):
    for ib in range(N_I * LANES // BI):
        at = slice(ib * BI, (ib + 1) * BI)
        dots = jnp.dot(right[...], left[:, at], preferred_element_type=f32)
        sq = jnp.concatenate([sq_j[...]] * (BI // LANES), axis=1)
        power = jnp.minimum(dots + sq_i[0:1, at] + sq, 0.0)
        kern = jnp.exp2(power)
        kh, kl = halves(kern)
        dh, dl = halves(kern * power)
        b, d, bl, dl = (jnp.dot(rhs[...], m, preferred_element_type=f32) for m in (kh, dh, kl, dl))
        b, d = b + bl, d + dl
        b = b[0:RHS] + b[HALF : HALF + RHS]
        d = d[0:PROBES] + d[HALF : HALF + PROBES]
        both = jnp.concatenate([b, d], axis=0)
        for p in range(BI // LANES):
            t = ib * (BI // LANES) + p
            part = both[:, p * LANES : (p + 1) * LANES]
            out_ref[t] = part if acc_ref is None else acc_ref[t] + part


def first_kernel(ls_ref, os_ref, noise_ref, me_ref, *refs):
    xi_refs, xj_ref, (out_ref, left, sq_i, params_ref), scratch = refs[:4], refs[4], refs[5:9], refs[9:]
    ell = ls_ref[0]
    c = (0.5 * LOG2E) / (ell * ell)
    for row, value in enumerate((c, os_ref[0], noise_ref[0], (-2.0 * math.log(2.0)) * os_ref[0] / ell)):
        params_ref[row : row + 1] = jnp.full((1, LANES), value, f32)
    prepare_j(c, xj_ref, *scratch)
    for s in range(4):
        for t in range(4):
            hi, lo = halves(xi_refs[s][t])
            x = hi.astype(f32) + lo.astype(f32)
            yh, yl = halves((2.0 * c) * x)
            at = tile(jnp.bitwise_xor(4 * s + t, me_ref[0]))
            left[0:64, at] = yh
            left[64:128, at] = yl
            left[128:192, at] = yh
            left[192:256, at] = yl
            sq_i[:, at] = jnp.broadcast_to(-c * jnp.sum(x * x, axis=0, keepdims=True), (8, LANES))
    blocks(left, sq_i, *scratch, None, out_ref)


def second_kernel(acc_ref, left, sq_i, params_ref, xj_ref, out_ref, *scratch):
    prepare_j(params_ref[0:1], xj_ref, *scratch)
    blocks(left, sq_i, *scratch, acc_ref, out_ref)


def products_call(kernel, out_shape, in_specs, out_specs, name):
    rows, cols = N_I * LANES, N_J * LANES
    return pl.pallas_call(
        kernel,
        out_shape=out_shape,
        in_specs=in_specs,
        out_specs=out_specs,
        scratch_shapes=[
            pltpu.VMEM((cols, 256), bf16),
            pltpu.VMEM((cols, LANES), f32),
            pltpu.VMEM((2 * HALF, cols), bf16),
        ],
        compiler_params=small(PRODUCTS_MIB),
        cost_estimate=pl.CostEstimate(flops=2 * rows * cols * 1280, bytes_accessed=2 << 20, transcendentals=rows * cols),
        name=name,
    )


def first_products(lengthscale, outputscale, noise, me, pieces, xj):
    rows = N_I * LANES
    out_shape = [shaped(N_I, BACK, LANES), shaped(256, rows, dtype=bf16), shaped(8, rows), shaped(8, LANES)]
    call = products_call(first_kernel, out_shape, [SMEM] * 4 + [VMEM] * 5, [VMEM] * 4, "first_products")
    return call(lengthscale, outputscale, noise, me, *pieces, xj)


def second_products(acc, left, sq_i, params, xj):
    call = products_call(second_kernel, shaped(N_I, BACK, LANES), [VMEM] * 5, VMEM, "second_products")
    return call(acc, left, sq_i, params, xj)


def sums_kernel(params_ref, rhs_ref, part_ref, lp_ref, sp_ref, off_ref, stat_ref):
    total = part_ref[0]
    for s in range(1, N_I):
        total = total + part_ref[s]
    eb = total[0:RHS]
    sp_ref[...] = eb[0:PROBES]
    lp_ref[...] = total[RHS:BACK] * params_ref[3:4]
    rhs = rhs_ref[...]
    off = eb - rhs
    off_ref[...] = off
    stacked = jnp.concatenate([rhs * rhs, rhs * off, off * off, jnp.zeros((8, LANES), f32)], axis=0)
    stat_ref[...] = jnp.broadcast_to(jnp.sum(stacked.T, axis=0, keepdims=True), (N_FIRST, LANES))


def sums(params, rhs, parts):
    return pl.pallas_call(
        sums_kernel,
        out_shape=[shaped(PROBES, LANES), shaped(PROBES, LANES), shaped(RHS, LANES), shaped(N_FIRST, LANES)],
        in_specs=[VMEM] * 3,
        out_specs=[VMEM] * 4,
        compiler_params=small(),
        name="sums",
    )(params, rhs, parts)


def again_kernel(stats_ref, out_ref):
    out_ref[...] = jnp.broadcast_to(jnp.sum(stats_ref[...], axis=0, keepdims=True), (N_LAST, LANES))


def again(stats):
    return pl.pallas_call(
        again_kernel, out_shape=shaped(N_LAST, LANES), in_specs=[VMEM], out_specs=VMEM, compiler_params=small(), name="again"
    )(stats)


def step_kernel(params_ref, rhs_ref, off_ref, stats_ref, sol_ref, res_ref, dir_ref):
    scale, noise = params_ref[1:2], params_ref[2:3]
    row = jnp.sum(stats_ref[...], axis=0, keepdims=True)
    column = jnp.broadcast_to(row, (LANES, LANES)).T
    rr, rg, gg = column[0:RHS], column[RHS : 2 * RHS], column[2 * RHS : 3 * RHS]
    rhs, off = rhs_ref[...], off_ref[...]
    curv = (scale + noise) * rr + scale * rg
    share = scale / curv
    sol = (rr / curv) * rhs
    res = share * (rg * rhs - rr * off)
    direction = res + (share * share * (rr * gg - rg * rg)) * rhs
    for ref, value in ((sol_ref, sol), (res_ref, res), (dir_ref, direction)):
        ref[0:1] = value[32:33]
        ref[1:33] = value[0:32]


def step(params, rhs, off, stats):
    return pl.pallas_call(
        step_kernel,
        out_shape=[shaped(PROBES + 1, LANES)] * 3,
        in_specs=[VMEM] * 4,
        out_specs=[VMEM] * 3,
        compiler_params=small(),
        name="step",
    )(params, rhs, off, stats)


def exchange(x, axes):
    return lax.all_to_all(x, axes, 0, 0, tiled=True)


def swap(x, axis):
    return lax.ppermute(x, axis, [(0, 1), (1, 0)])


def others(x, axes):
    return [lax.ppermute(x, axes, [(i, i ^ m) for i in range(4)]) for m in (1, 2, 3)]


def shards(points, targets, probes, lengthscale, outputscale, noise):
    to_j, rhs = pack(points, probes, targets)
    xa = exchange(to_j, J_GROUP)
    near = jnp.stack([points] + others(points, I_GROUP[2:]))
    pieces = [near] + others(near, I_GROUP[:2])
    xb = swap(xa, "co")
    me = lax.axis_index(I_GROUP).reshape(1)
    half, left, sq_i, params = first_products(lengthscale, outputscale, noise, me, pieces, xa)
    parts = exchange(second_products(half, left, sq_i, params, xb), I_GROUP)
    lp, sp, off, stat = sums(params, rhs, parts)
    stats = exchange(again(exchange(stat, SUM_FIRST)), SUM_LAST)
    sol, res, direction = step(params, rhs, off, stats)
    return sol, res, direction, lp, sp


def solution(mesh):
    apart = Mesh(mesh.devices.reshape(SIZES), AXES)
    split = P(None, AXES)
    return jax.shard_map(
        shards,
        mesh=apart,
        in_specs=(split, P(AXES), split, P(), P(), P()),
        out_specs=(split,) * 5,
        check_vma=False,
    )
```

time: 124 us -> 116 us (0.935)
  blocking collectives: 15.3 us -> 41 us
  waiting for transfers between devices: 30.4 us -> 8.29 us
  starting transfers between devices: 50 us -> 39.8 us
  Pallas kernels: 25.1 us -> 23.3 us
    all_to_all x1 -> x3, blocking collectives: 15.3 us -> 41 us  [exchange(): return lax.all_to_all(x, axes, 0, 0, tiled=True)]
    ppermute x0 -> x6, starting transfers between devices: none -> 17.4 us  [others(): lax.ppermute(x, axes, [(i, i ^ m) for i in range(4)])]
    all_to_all x3 -> x1, starting transfers between devices: 30.9 us -> 16.4 us  [exchange(): return lax.all_to_all(x, axes, 0, 0, tiled=True)]
    ppermute x5 -> x1, waiting for transfers between devices: 13.3 us -> 0.01 us  [swap(): return lax.ppermute(x, axis, [(0, 1), (1, 0)])]
    ppermute x5 -> x1, starting transfers between devices: 19.1 us -> 6.11 us  [swap(): return lax.ppermute(x, axis, [(0, 1), (1, 0)])]
    all_to_all x3 -> x1, waiting for transfers between devices: 17.1 us -> 5.5 us  [exchange(): return lax.all_to_all(x, axes, 0, 0, tiled=True)]
    ppermute x0 -> x6, waiting for transfers between devices: none -> 2.78 us  [others(): lax.ppermute(x, axes, [(i, i ^ m) for i in range(4)])]
  transfers between devices with their start and end apart: 8 -> 8, of which waited for: 5 -> 3; matrix products, arithmetic and copies ran while one was open for 0% -> 0% of each run, Pallas kernels for 8% -> 9%
where the time goes in v3:
time: 116 us; the launch traced here: 115 us
  blocking collectives  41 us (35%)
  starting transfers between devices  39.8 us (34%)
  Pallas kernels  23.3 us (20%)
  waiting for transfers between devices  8.29 us (7%)
  between operations  2.73 us (2%)
    all_to_all x3, blocking collectives, exchange(): return lax.all_to_all(x, axes, 0, 0, tiled=True)  41 us
    ppermute x6, starting transfers between devices, others(): lax.ppermute(x, axes, [(i, i ^ m) for i in range(4)])  17.4 us
    all_to_all x1, starting transfers between devices, exchange(): return lax.all_to_all(x, axes, 0, 0, tiled=True)  16.4 us
    pallas_call x1, Pallas kernels, second_products(): return call(acc, left, sq_i, params, xj)  10.1 us
    pallas_call x1, Pallas kernels, first_products(): return call(lengthscale, outputscale, noise, me, *pieces, xj)  10.1 us
    ppermute x1, starting transfers between devices, swap(): return lax.ppermute(x, axis, [(0, 1), (1, 0)])  6.11 us
    all_to_all x1, waiting for transfers between devices, exchange(): return lax.all_to_all(x, axes, 0, 0, tiled=True)  5.5 us
    ppermute x6, waiting for transfers between devices, others(): lax.ppermute(x, axes, [(i, i ^ m) for i in range(4)])  2.78 us
  transfers between devices with their start and end apart: 8, of which 3 were waited for; matrix products, arithmetic and copies ran while one was open for 0% of the time, Pallas kernels for 9%

profile of v3, /device:TPU:1, one launch (start us, length us, event | category | flops | bytes accessed | tf_op | source)
XLA Modules:
  0.0 115.2 jit_solution(14568581381038303120)
XLA Ops:
  0.6 1.8 %pack.1 = (f32[16,104,128]{2,1,0:T(8,128)}, f32[40,128]{1,0:T(8,128)}) custom-call(f32[64,128]{1,0:T(8,128)} %points_ref.1, f32[32,128]{1,0:T(8,128)} %probes_ref.1, f32[1,128]{1,0:T(1,128)} %bitcast.22), custom_call_target="tpu_custom_call" | custom-call | bytes 2097152 | tf_op jit(solution)/shard_map/pack/pallas_call | solution.py:63
  2.4 0.0 copy-start.1
  2.4 16.4 %all-to-all-start = ((f32[16,104,128]{2,1,0:T(8,128)}), f32[16,104,128]{2,1,0:T(8,128)S(1)}, u32[]{:S(2)}, u32[]{:S(2)}) async-start(f32[16,104,128]{2,1,0:T(8,128)} %get-tuple-element.18), calls=%async_computation | async-start | bytes 1703936 | tf_op jit(solution)/shard_map/all_to_all | solution.py:231
  18.7 0.0 copy-done.1
  18.8 4.4 %collective-permute-start.2 = (f32[64,128]{1,0:T(8,128)S(1)}, f32[64,128]{1,0:T(8,128)S(1)}, u32[]{:S(2)}, u32[]{:S(2)}) collective-permute-start(f32[64,128]{1,0:T(8,128)S(1)} %copy-done.1), channel_id=1, source_target_pairs={{0,258},{2,256},{256,2},{258,0},{1,259},{3,257},{257,3},{259,1},{4... | collective-permute-start | bytes 98312 | tf_op jit(solution)/shard_map/ppermute | solution.py:239
  23.1 2.4 %collective-permute-start.1 = (f32[64,128]{1,0:T(8,128)S(1)}, f32[64,128]{1,0:T(8,128)S(1)}, u32[]{:S(2)}, u32[]{:S(2)}) collective-permute-start(f32[64,128]{1,0:T(8,128)S(1)} %copy-done.1), channel_id=1, source_target_pairs={{0,256},{2,258},{256,0},{258,2},{1,257},{3,259},{257,1},{259,3},{4... | collective-permute-start | bytes 98312 | tf_op jit(solution)/shard_map/ppermute | solution.py:239
  25.6 2.2 %collective-permute-start = (f32[64,128]{1,0:T(8,128)S(1)}, f32[64,128]{1,0:T(8,128)S(1)}, u32[]{:S(2)}, u32[]{:S(2)}) collective-permute-start(f32[64,128]{1,0:T(8,128)S(1)} %copy-done.1), channel_id=1, source_target_pairs={{0,2},{2,0},{256,258},{258,256},{1,3},{3,1},{257,259},{259,257},{4... | collective-permute-start | bytes 98312 | tf_op jit(solution)/shard_map/ppermute | solution.py:239
  27.8 0.0 collective-permute-done.2
  27.8 1.5 %collective-permute-done.1 = f32[64,128]{1,0:T(8,128)S(1)} collective-permute-done((f32[64,128]{1,0:T(8,128)S(1)}, f32[64,128]{1,0:T(8,128)S(1)}, u32[]{:S(2)}, u32[]{:S(2)}) %collective-permute-start.1) | collective-permute-done | bytes 32800 | tf_op jit(solution)/shard_map/ppermute | solution.py:239
  29.3 1.2 %collective-permute-done = f32[64,128]{1,0:T(8,128)S(1)} collective-permute-done((f32[64,128]{1,0:T(8,128)S(1)}, f32[64,128]{1,0:T(8,128)S(1)}, u32[]{:S(2)}, u32[]{:S(2)}) %collective-permute-start) | collective-permute-done | bytes 32800 | tf_op jit(solution)/shard_map/ppermute | solution.py:239
  30.6 2.3 %collective-permute-start.3 = (f32[4,64,128]{2,1,0:T(8,128)S(1)}, f32[4,64,128]{2,1,0:T(8,128)S(1)}, u32[]{:S(2)}, u32[]{:S(2)}) collective-permute-start(f32[4,64,128]{2,1,0:T(8,128)S(1)} %pad_maximum_fusion.refs_0_), channel_id=1, source_target_pairs={{0,4},{4,0},{32,36},{36,32},{1,5},{5,1},{33,37},{37,33},{2,6},{6,2... | collective-permute-start | bytes 393224 | tf_op jit(solution)/shard_map/ppermute | solution.py:239
  32.9 3.1 %collective-permute-start.4 = (f32[4,64,128]{2,1,0:T(8,128)S(1)}, f32[4,64,128]{2,1,0:T(8,128)S(1)}, u32[]{:S(2)}, u32[]{:S(2)}) collective-permute-start(f32[4,64,128]{2,1,0:T(8,128)S(1)} %pad_maximum_fusion.refs_0_), channel_id=1, source_target_pairs={{0,32},{4,36},{32,0},{36,4},{1,33},{5,37},{33,1},{37,5},{2,34},{6,... | collective-permute-start | bytes 393224 | tf_op jit(solution)/shard_map/ppermute | solution.py:239
  36.0 3.0 %collective-permute-start.5 = (f32[4,64,128]{2,1,0:T(8,128)S(1)}, f32[4,64,128]{2,1,0:T(8,128)S(1)}, u32[]{:S(2)}, u32[]{:S(2)}) collective-permute-start(f32[4,64,128]{2,1,0:T(8,128)S(1)} %pad_maximum_fusion.refs_0_), channel_id=1, source_target_pairs={{0,36},{4,32},{32,4},{36,0},{1,37},{5,33},{33,5},{37,1},{2,38},{6,... | collective-permute-start | bytes 393224 | tf_op jit(solution)/shard_map/ppermute | solution.py:239
  40.9 5.5 %all-to-all-done.refs_4_ = f32[16,104,128]{2,1,0:T(8,128)S(1)} async-done(((f32[16,104,128]{2,1,0:T(8,128)}), f32[16,104,128]{2,1,0:T(8,128)S(1)}, u32[]{:S(2)}, u32[]{:S(2)}) %all-to-all-start) | async-done | bytes 852000 | tf_op jit(solution)/shard_map/all_to_all | solution.py:231
  46.4 6.1 %collective-permute-start.6 = (f32[16,104,128]{2,1,0:T(8,128)S(1)}, f32[16,104,128]{2,1,0:T(8,128)S(1)}, u32[]{:S(2)}, u32[]{:S(2)}) collective-permute-start(f32[16,104,128]{2,1,0:T(8,128)S(1)} %all-to-all-done.refs_4_), channel_id=1, source_target_pairs={{0,1},{1,0},{2,3},{3,2},{4,5},{5,4},{6,7},{7,6},{8,9},{9,8},{10,11... | collective-permute-start | bytes 2555912 | tf_op jit(solution)/shard_map/ppermute | solution.py:235
  52.5 0.0 collective-permute-done.3.refs_1_
  52.5 0.0 collective-permute-done.4.refs_2_
  52.5 0.0 collective-permute-done.5.refs_3_
  52.6 10.1 %first_products.1 = (f32[16,72,128]{2,1,0:T(8,128)S(1)}, bf16[256,2048]{1,0:T(8,128)(2,1)S(1)}, f32[8,2048]{1,0:T(8,128)S(1)}, f32[8,128]{1,0:T(8,128)S(1)}) custom-call(f32[1]{0:T(128)S(6)} %copy.13.ls_ref, f32[1]{0:T(128)S(6)} %copy.14.os_ref, f32[1]{0:T(128)S(6)} %copy.15.noise_ref, s32[1]{0:T(128)} %bitcast.me_ref, ...), custom_call_target="tpu_custom_call" | custom-call | flops 10737418240 | bytes 2097152 | tf_op jit(solution)/shard_map/first_products/pallas_call | solution.py:160
  62.6 0.0 collective-permute-done.6.xj_ref
  62.6 10.1 %second_products.1 = f32[16,72,128]{2,1,0:T(8,128)S(1)} custom-call(f32[16,72,128]{2,1,0:T(8,128)S(1)} %get-tuple-element.21.acc_ref, bf16[256,2048]{1,0:T(8,128)(2,1)S(1)} %get-tuple-element.22.left, f32[8,2048]{1,0:T(8,128)S(1)} %get-tuple-element.23.sq_i, f32[8,128]{1,0:T(8,128)S(1)} %get-tuple-element.19.params_ref, ...), custom_call_target="tpu_custom_call" | custom-call | flops 10737418240 | bytes 2097152 | tf_op jit(solution)/shard_map/second_products/pallas_call | solution.py:165
  72.7 0.0 copy-start
  72.7 15.7 %all_to_all.32.part_ref = f32[16,72,128]{2,1,0:T(8,128)S(1)} all-to-all(f32[16,72,128]{2,1,0:T(8,128)S(1)} %second_products.1), channel_id=1, replica_groups=mesh['xh'=2,'zh'=2,'zm'=2,'za'=2,'yb'=4,'ya'=2,'xl'=2,'co'=2] {'za','ya'..., dimensions={0} | all-to-all | bytes 1179648 | tf_op jit(solution)/shard_map/all_to_all | solution.py:231
  88.5 0.0 copy-done
  88.5 0.7 sums.1
  89.2 10.8 %all_to_all.33 = f32[16,1,128]{2,1,0:T(1,128)S(1)} all-to-all(f32[16,1,128]{2,1,0:T(1,128)S(1)} %bitcast.17), channel_id=1, replica_groups=mesh['xh'=2,'zh'=2,'zm'=2,'za'=2,'yb'=4,'ya'=2,'xl'=2,'co'=2] {'yb','ya'..., dimensions={0} | all-to-all | bytes 16384 | tf_op jit(solution)/shard_map/all_to_all | solution.py:231
  100.0 14.4 %all_to_all.34 = f32[32,1,128]{2,1,0:T(1,128)S(1)} all-to-all(f32[32,1,128]{2,1,0:T(1,128)S(1)} %bitcast.14), channel_id=1, replica_groups=mesh['xh'=2,'zh'=2,'zm'=2,'za'=2,'yb'=4,'ya'=2,'xl'=2,'co'=2] {'xh','xl'..., dimensions={0} | all-to-all | bytes 32768 | tf_op jit(solution)/shard_map/all_to_all | solution.py:231
  114.4 0.7 step.1
  (2 shorter events, 0.0 us)
Async XLA Ops:
  2.4 16.4 %copy-start.1 = (f32[64,128]{1,0:T(8,128)S(1)}, f32[64,128]{1,0:T(8,128)}, u32[]{:S(2)}) copy-start(f32[64,128]{1,0:T(8,128)} %points_ref.1) | copy-start | bytes 98308
  2.4 44.0 %all-to-all-start = ((f32[16,104,128]{2,1,0:T(8,128)}), f32[16,104,128]{2,1,0:T(8,128)S(1)}, u32[]{:S(2)}, u32[]{:S(2)}) async-start(f32[16,104,128]{2,1,0:T(8,128)} %get-tuple-element.18), calls=%async_computation | async-start | bytes 1703936 | tf_op jit(solution)/shard_map/all_to_all | solution.py:231
  18.8 9.0 %collective-permute-start.2 = (f32[64,128]{1,0:T(8,128)S(1)}, f32[64,128]{1,0:T(8,128)S(1)}, u32[]{:S(2)}, u32[]{:S(2)}) collective-permute-start(f32[64,128]{1,0:T(8,128)S(1)} %copy-done.1), channel_id=1, source_target_pairs={{0,258},{2,256},{256,2},{258,0},{1,259},{3,257},{257,3},{259,1},{4... | collective-permute-start | bytes 98312 | tf_op jit(solution)/shard_map/ppermute | solution.py:239
  23.1 6.2 %collective-permute-start.1 = (f32[64,128]{1,0:T(8,128)S(1)}, f32[64,128]{1,0:T(8,128)S(1)}, u32[]{:S(2)}, u32[]{:S(2)}) collective-permute-start(f32[64,128]{1,0:T(8,128)S(1)} %copy-done.1), channel_id=1, source_target_pairs={{0,256},{2,258},{256,0},{258,2},{1,257},{3,259},{257,1},{259,3},{4... | collective-permute-start | bytes 98312 | tf_op jit(solution)/shard_map/ppermute | solution.py:239
  25.6 5.0 %collective-permute-start = (f32[64,128]{1,0:T(8,128)S(1)}, f32[64,128]{1,0:T(8,128)S(1)}, u32[]{:S(2)}, u32[]{:S(2)}) collective-permute-start(f32[64,128]{1,0:T(8,128)S(1)} %copy-done.1), channel_id=1, source_target_pairs={{0,2},{2,0},{256,258},{258,256},{1,3},{3,1},{257,259},{259,257},{4... | collective-permute-start | bytes 98312 | tf_op jit(solution)/shard_map/ppermute | solution.py:239
  30.6 22.0 %collective-permute-start.3 = (f32[4,64,128]{2,1,0:T(8,128)S(1)}, f32[4,64,128]{2,1,0:T(8,128)S(1)}, u32[]{:S(2)}, u32[]{:S(2)}) collective-permute-start(f32[4,64,128]{2,1,0:T(8,128)S(1)} %pad_maximum_fusion.refs_0_), channel_id=1, source_target_pairs={{0,4},{4,0},{32,36},{36,32},{1,5},{5,1},{33,37},{37,33},{2,6},{6,2... | collective-permute-start | bytes 393224 | tf_op jit(solution)/shard_map/ppermute | solution.py:239
  32.9 19.7 %collective-permute-start.4 = (f32[4,64,128]{2,1,0:T(8,128)S(1)}, f32[4,64,128]{2,1,0:T(8,128)S(1)}, u32[]{:S(2)}, u32[]{:S(2)}) collective-permute-start(f32[4,64,128]{2,1,0:T(8,128)S(1)} %pad_maximum_fusion.refs_0_), channel_id=1, source_target_pairs={{0,32},{4,36},{32,0},{36,4},{1,33},{5,37},{33,1},{37,5},{2,34},{6,... | collective-permute-start | bytes 393224 | tf_op jit(solution)/shard_map/ppermute | solution.py:239
  36.0 16.6 %collective-permute-start.5 = (f32[4,64,128]{2,1,0:T(8,128)S(1)}, f32[4,64,128]{2,1,0:T(8,128)S(1)}, u32[]{:S(2)}, u32[]{:S(2)}) collective-permute-start(f32[4,64,128]{2,1,0:T(8,128)S(1)} %pad_maximum_fusion.refs_0_), channel_id=1, source_target_pairs={{0,36},{4,32},{32,4},{36,0},{1,37},{5,33},{33,5},{37,1},{2,38},{6,... | collective-permute-start | bytes 393224 | tf_op jit(solution)/shard_map/ppermute | solution.py:239
  46.4 16.2 %collective-permute-start.6 = (f32[16,104,128]{2,1,0:T(8,128)S(1)}, f32[16,104,128]{2,1,0:T(8,128)S(1)}, u32[]{:S(2)}, u32[]{:S(2)}) collective-permute-start(f32[16,104,128]{2,1,0:T(8,128)S(1)} %all-to-all-done.refs_4_), channel_id=1, source_target_pairs={{0,1},{1,0},{2,3},{3,2},{4,5},{5,4},{6,7},{7,6},{8,9},{9,8},{10,11... | collective-permute-start | bytes 2555912 | tf_op jit(solution)/shard_map/ppermute | solution.py:235
  72.7 15.8 %copy-start = (f32[40,128]{1,0:T(8,128)S(1)}, f32[40,128]{1,0:T(8,128)}, u32[]{:S(2)}) copy-start(f32[40,128]{1,0:T(8,128)} %get-tuple-element.20.rhs_ref) | copy-start | bytes 61444

commit v4 on v3

--- a/solution.py
+++ b/solution.py
@@ -10,7 +10,7 @@
 AXES = ("xh", "zh", "zm", "za", "yb", "ya", "xl", "co")
 SIZES = (2, 2, 2, 2, 4, 2, 2, 2)
 I_GROUP = ("za", "ya", "xh", "xl")
-J_GROUP = ("yb", "zh", "zm")
+J_GROUP = ("zh", "zm", "yb")
 SUM_FIRST = ("yb", "ya", "co")
 SUM_LAST = ("xh", "xl", "zh", "zm", "za")
 N_I = 16

time: 116 us -> 116 us (level)
  blocking collectives: 41 us -> 43.8 us
  waiting for transfers between devices: 8.29 us -> 5.99 us
    all_to_all x3, blocking collectives: 41 us -> 43.8 us  [exchange(): return lax.all_to_all(x, axes, 0, 0, tiled=True)]
    all_to_all x1, waiting for transfers between devices: 5.5 us -> 3.21 us  [exchange(): return lax.all_to_all(x, axes, 0, 0, tiled=True)]
where the time goes in v4:
time: 116 us; the launch traced here: 115 us
  blocking collectives  43.8 us (38%)
  starting transfers between devices  39.2 us (34%)
  Pallas kernels  23.3 us (20%)
  waiting for transfers between devices  5.99 us (5%)
  between operations  2.73 us (2%)
    all_to_all x3, blocking collectives, exchange(): return lax.all_to_all(x, axes, 0, 0, tiled=True)  43.8 us
    ppermute x6, starting transfers between devices, others(): lax.ppermute(x, axes, [(i, i ^ m) for i in range(4)])  17.4 us
    all_to_all x1, starting transfers between devices, exchange(): return lax.all_to_all(x, axes, 0, 0, tiled=True)  16.4 us
    pallas_call x1, Pallas kernels, second_products(): return call(acc, left, sq_i, params, xj)  10.1 us
    pallas_call x1, Pallas kernels, first_products(): return call(lengthscale, outputscale, noise, me, *pieces, xj)  10 us
    ppermute x1, starting transfers between devices, swap(): return lax.ppermute(x, axis, [(0, 1), (1, 0)])  5.52 us
    all_to_all x1, waiting for transfers between devices, exchange(): return lax.all_to_all(x, axes, 0, 0, tiled=True)  3.21 us
    ppermute x6, waiting for transfers between devices, others(): lax.ppermute(x, axes, [(i, i ^ m) for i in range(4)])  2.78 us
  transfers between devices with their start and end apart: 8, of which 3 were waited for; matrix products, arithmetic and copies ran while one was open for 0% of the time, Pallas kernels for 9%

profile of v4, /device:TPU:1, one launch (start us, length us, event | category | flops | bytes accessed | tf_op | source)
XLA Modules:
  0.0 115.0 jit_solution(9000787823240193018)
XLA Ops:
  0.6 1.8 %pack.1 = (f32[16,104,128]{2,1,0:T(8,128)}, f32[40,128]{1,0:T(8,128)}) custom-call(f32[64,128]{1,0:T(8,128)} %points_ref.1, f32[32,128]{1,0:T(8,128)} %probes_ref.1, f32[1,128]{1,0:T(1,128)} %bitcast.22), custom_call_target="tpu_custom_call" | custom-call | bytes 2097152 | tf_op jit(solution)/shard_map/pack/pallas_call | solution.py:63
  2.4 0.0 copy-start.1
  2.4 16.4 %all-to-all-start = ((f32[16,104,128]{2,1,0:T(8,128)}), f32[16,104,128]{2,1,0:T(8,128)S(1)}, u32[]{:S(2)}, u32[]{:S(2)}) async-start(f32[16,104,128]{2,1,0:T(8,128)} %get-tuple-element.18), calls=%async_computation | async-start | bytes 1703936 | tf_op jit(solution)/shard_map/all_to_all | solution.py:231
  18.7 0.0 copy-done.1
  18.8 4.4 %collective-permute-start.2 = (f32[64,128]{1,0:T(8,128)S(1)}, f32[64,128]{1,0:T(8,128)S(1)}, u32[]{:S(2)}, u32[]{:S(2)}) collective-permute-start(f32[64,128]{1,0:T(8,128)S(1)} %copy-done.1), channel_id=1, source_target_pairs={{0,258},{2,256},{256,2},{258,0},{1,259},{3,257},{257,3},{259,1},{4... | collective-permute-start | bytes 98312 | tf_op jit(solution)/shard_map/ppermute | solution.py:239
  23.1 2.4 %collective-permute-start.1 = (f32[64,128]{1,0:T(8,128)S(1)}, f32[64,128]{1,0:T(8,128)S(1)}, u32[]{:S(2)}, u32[]{:S(2)}) collective-permute-start(f32[64,128]{1,0:T(8,128)S(1)} %copy-done.1), channel_id=1, source_target_pairs={{0,256},{2,258},{256,0},{258,2},{1,257},{3,259},{257,1},{259,3},{4... | collective-permute-start | bytes 98312 | tf_op jit(solution)/shard_map/ppermute | solution.py:239
  25.6 2.2 %collective-permute-start = (f32[64,128]{1,0:T(8,128)S(1)}, f32[64,128]{1,0:T(8,128)S(1)}, u32[]{:S(2)}, u32[]{:S(2)}) collective-permute-start(f32[64,128]{1,0:T(8,128)S(1)} %copy-done.1), channel_id=1, source_target_pairs={{0,2},{2,0},{256,258},{258,256},{1,3},{3,1},{257,259},{259,257},{4... | collective-permute-start | bytes 98312 | tf_op jit(solution)/shard_map/ppermute | solution.py:239
  27.8 0.0 collective-permute-done.2
  27.8 1.8 %collective-permute-done.1 = f32[64,128]{1,0:T(8,128)S(1)} collective-permute-done((f32[64,128]{1,0:T(8,128)S(1)}, f32[64,128]{1,0:T(8,128)S(1)}, u32[]{:S(2)}, u32[]{:S(2)}) %collective-permute-start.1) | collective-permute-done | bytes 32800 | tf_op jit(solution)/shard_map/ppermute | solution.py:239
  29.6 0.9 collective-permute-done
  30.6 2.3 %collective-permute-start.3 = (f32[4,64,128]{2,1,0:T(8,128)S(1)}, f32[4,64,128]{2,1,0:T(8,128)S(1)}, u32[]{:S(2)}, u32[]{:S(2)}) collective-permute-start(f32[4,64,128]{2,1,0:T(8,128)S(1)} %pad_maximum_fusion.refs_0_), channel_id=1, source_target_pairs={{0,4},{4,0},{32,36},{36,32},{1,5},{5,1},{33,37},{37,33},{2,6},{6,2... | collective-permute-start | bytes 393224 | tf_op jit(solution)/shard_map/ppermute | solution.py:239
  32.9 3.1 %collective-permute-start.4 = (f32[4,64,128]{2,1,0:T(8,128)S(1)}, f32[4,64,128]{2,1,0:T(8,128)S(1)}, u32[]{:S(2)}, u32[]{:S(2)}) collective-permute-start(f32[4,64,128]{2,1,0:T(8,128)S(1)} %pad_maximum_fusion.refs_0_), channel_id=1, source_target_pairs={{0,32},{4,36},{32,0},{36,4},{1,33},{5,37},{33,1},{37,5},{2,34},{6,... | collective-permute-start | bytes 393224 | tf_op jit(solution)/shard_map/ppermute | solution.py:239
  36.0 3.0 %collective-permute-start.5 = (f32[4,64,128]{2,1,0:T(8,128)S(1)}, f32[4,64,128]{2,1,0:T(8,128)S(1)}, u32[]{:S(2)}, u32[]{:S(2)}) collective-permute-start(f32[4,64,128]{2,1,0:T(8,128)S(1)} %pad_maximum_fusion.refs_0_), channel_id=1, source_target_pairs={{0,36},{4,32},{32,4},{36,0},{1,37},{5,33},{33,5},{37,1},{2,38},{6,... | collective-permute-start | bytes 393224 | tf_op jit(solution)/shard_map/ppermute | solution.py:239
  40.9 3.2 %all-to-all-done.refs_4_ = f32[16,104,128]{2,1,0:T(8,128)S(1)} async-done(((f32[16,104,128]{2,1,0:T(8,128)}), f32[16,104,128]{2,1,0:T(8,128)S(1)}, u32[]{:S(2)}, u32[]{:S(2)}) %all-to-all-start) | async-done | bytes 852000 | tf_op jit(solution)/shard_map/all_to_all | solution.py:231
  44.1 5.5 %collective-permute-start.6 = (f32[16,104,128]{2,1,0:T(8,128)S(1)}, f32[16,104,128]{2,1,0:T(8,128)S(1)}, u32[]{:S(2)}, u32[]{:S(2)}) collective-permute-start(f32[16,104,128]{2,1,0:T(8,128)S(1)} %all-to-all-done.refs_4_), channel_id=1, source_target_pairs={{0,1},{1,0},{2,3},{3,2},{4,5},{5,4},{6,7},{7,6},{8,9},{9,8},{10,11... | collective-permute-start | bytes 2555912 | tf_op jit(solution)/shard_map/ppermute | solution.py:235
  49.6 0.0 collective-permute-done.3.refs_1_
  49.6 0.0 collective-permute-done.4.refs_2_
  49.7 0.0 collective-permute-done.5.refs_3_
  49.7 10.0 %first_products.1 = (f32[16,72,128]{2,1,0:T(8,128)S(1)}, bf16[256,2048]{1,0:T(8,128)(2,1)S(1)}, f32[8,2048]{1,0:T(8,128)S(1)}, f32[8,128]{1,0:T(8,128)S(1)}) custom-call(f32[1]{0:T(128)S(6)} %copy.13.ls_ref, f32[1]{0:T(128)S(6)} %copy.14.os_ref, f32[1]{0:T(128)S(6)} %copy.15.noise_ref, s32[1]{0:T(128)} %bitcast.me_ref, ...), custom_call_target="tpu_custom_call" | custom-call | flops 10737418240 | bytes 2097152 | tf_op jit(solution)/shard_map/first_products/pallas_call | solution.py:160
  59.7 0.0 collective-permute-done.6.xj_ref
  59.8 10.1 %second_products.1 = f32[16,72,128]{2,1,0:T(8,128)S(1)} custom-call(f32[16,72,128]{2,1,0:T(8,128)S(1)} %get-tuple-element.21.acc_ref, bf16[256,2048]{1,0:T(8,128)(2,1)S(1)} %get-tuple-element.22.left, f32[8,2048]{1,0:T(8,128)S(1)} %get-tuple-element.23.sq_i, f32[8,128]{1,0:T(8,128)S(1)} %get-tuple-element.19.params_ref, ...), custom_call_target="tpu_custom_call" | custom-call | flops 10737418240 | bytes 2097152 | tf_op jit(solution)/shard_map/second_products/pallas_call | solution.py:165
  69.8 0.0 copy-start
  69.9 16.3 %all_to_all.32.part_ref = f32[16,72,128]{2,1,0:T(8,128)S(1)} all-to-all(f32[16,72,128]{2,1,0:T(8,128)S(1)} %second_products.1), channel_id=1, replica_groups=mesh['xh'=2,'zh'=2,'zm'=2,'za'=2,'yb'=4,'ya'=2,'xl'=2,'co'=2] {'za','ya'..., dimensions={0} | all-to-all | bytes 1179648 | tf_op jit(solution)/shard_map/all_to_all | solution.py:231
  86.1 0.0 copy-done
  86.1 0.7 sums.1
  86.8 14.1 %all_to_all.33 = f32[16,1,128]{2,1,0:T(1,128)S(1)} all-to-all(f32[16,1,128]{2,1,0:T(1,128)S(1)} %bitcast.17), channel_id=1, replica_groups=mesh['xh'=2,'zh'=2,'zm'=2,'za'=2,'yb'=4,'ya'=2,'xl'=2,'co'=2] {'yb','ya'..., dimensions={0} | all-to-all | bytes 16384 | tf_op jit(solution)/shard_map/all_to_all | solution.py:231
  100.9 13.4 %all_to_all.34 = f32[32,1,128]{2,1,0:T(1,128)S(1)} all-to-all(f32[32,1,128]{2,1,0:T(1,128)S(1)} %bitcast.14), channel_id=1, replica_groups=mesh['xh'=2,'zh'=2,'zm'=2,'za'=2,'yb'=4,'ya'=2,'xl'=2,'co'=2] {'xh','xl'..., dimensions={0} | all-to-all | bytes 32768 | tf_op jit(solution)/shard_map/all_to_all | solution.py:231
  114.3 0.7 step.1
  (2 shorter events, 0.0 us)
Async XLA Ops:
  2.4 16.4 %copy-start.1 = (f32[64,128]{1,0:T(8,128)S(1)}, f32[64,128]{1,0:T(8,128)}, u32[]{:S(2)}) copy-start(f32[64,128]{1,0:T(8,128)} %points_ref.1) | copy-start | bytes 98308
  2.4 41.7 %all-to-all-start = ((f32[16,104,128]{2,1,0:T(8,128)}), f32[16,104,128]{2,1,0:T(8,128)S(1)}, u32[]{:S(2)}, u32[]{:S(2)}) async-start(f32[16,104,128]{2,1,0:T(8,128)} %get-tuple-element.18), calls=%async_computation | async-start | bytes 1703936 | tf_op jit(solution)/shard_map/all_to_all | solution.py:231
  18.8 9.0 %collective-permute-start.2 = (f32[64,128]{1,0:T(8,128)S(1)}, f32[64,128]{1,0:T(8,128)S(1)}, u32[]{:S(2)}, u32[]{:S(2)}) collective-permute-start(f32[64,128]{1,0:T(8,128)S(1)} %copy-done.1), channel_id=1, source_target_pairs={{0,258},{2,256},{256,2},{258,0},{1,259},{3,257},{257,3},{259,1},{4... | collective-permute-start | bytes 98312 | tf_op jit(solution)/shard_map/ppermute | solution.py:239
  23.1 6.5 %collective-permute-start.1 = (f32[64,128]{1,0:T(8,128)S(1)}, f32[64,128]{1,0:T(8,128)S(1)}, u32[]{:S(2)}, u32[]{:S(2)}) collective-permute-start(f32[64,128]{1,0:T(8,128)S(1)} %copy-done.1), channel_id=1, source_target_pairs={{0,256},{2,258},{256,0},{258,2},{1,257},{3,259},{257,1},{259,3},{4... | collective-permute-start | bytes 98312 | tf_op jit(solution)/shard_map/ppermute | solution.py:239
  25.6 5.0 %collective-permute-start = (f32[64,128]{1,0:T(8,128)S(1)}, f32[64,128]{1,0:T(8,128)S(1)}, u32[]{:S(2)}, u32[]{:S(2)}) collective-permute-start(f32[64,128]{1,0:T(8,128)S(1)} %copy-done.1), channel_id=1, source_target_pairs={{0,2},{2,0},{256,258},{258,256},{1,3},{3,1},{257,259},{259,257},{4... | collective-permute-start | bytes 98312 | tf_op jit(solution)/shard_map/ppermute | solution.py:239
  30.6 19.1 %collective-permute-start.3 = (f32[4,64,128]{2,1,0:T(8,128)S(1)}, f32[4,64,128]{2,1,0:T(8,128)S(1)}, u32[]{:S(2)}, u32[]{:S(2)}) collective-permute-start(f32[4,64,128]{2,1,0:T(8,128)S(1)} %pad_maximum_fusion.refs_0_), channel_id=1, source_target_pairs={{0,4},{4,0},{32,36},{36,32},{1,5},{5,1},{33,37},{37,33},{2,6},{6,2... | collective-permute-start | bytes 393224 | tf_op jit(solution)/shard_map/ppermute | solution.py:239
  32.9 16.8 %collective-permute-start.4 = (f32[4,64,128]{2,1,0:T(8,128)S(1)}, f32[4,64,128]{2,1,0:T(8,128)S(1)}, u32[]{:S(2)}, u32[]{:S(2)}) collective-permute-start(f32[4,64,128]{2,1,0:T(8,128)S(1)} %pad_maximum_fusion.refs_0_), channel_id=1, source_target_pairs={{0,32},{4,36},{32,0},{36,4},{1,33},{5,37},{33,1},{37,5},{2,34},{6,... | collective-permute-start | bytes 393224 | tf_op jit(solution)/shard_map/ppermute | solution.py:239
  36.0 13.7 %collective-permute-start.5 = (f32[4,64,128]{2,1,0:T(8,128)S(1)}, f32[4,64,128]{2,1,0:T(8,128)S(1)}, u32[]{:S(2)}, u32[]{:S(2)}) collective-permute-start(f32[4,64,128]{2,1,0:T(8,128)S(1)} %pad_maximum_fusion.refs_0_), channel_id=1, source_target_pairs={{0,36},{4,32},{32,4},{36,0},{1,37},{5,33},{33,5},{37,1},{2,38},{6,... | collective-permute-start | bytes 393224 | tf_op jit(solution)/shard_map/ppermute | solution.py:239
  44.1 15.6 %collective-permute-start.6 = (f32[16,104,128]{2,1,0:T(8,128)S(1)}, f32[16,104,128]{2,1,0:T(8,128)S(1)}, u32[]{:S(2)}, u32[]{:S(2)}) collective-permute-start(f32[16,104,128]{2,1,0:T(8,128)S(1)} %all-to-all-done.refs_4_), channel_id=1, source_target_pairs={{0,1},{1,0},{2,3},{3,2},{4,5},{5,4},{6,7},{7,6},{8,9},{9,8},{10,11... | collective-permute-start | bytes 2555912 | tf_op jit(solution)/shard_map/ppermute | solution.py:235
  69.8 16.3 %copy-start = (f32[40,128]{1,0:T(8,128)S(1)}, f32[40,128]{1,0:T(8,128)}, u32[]{:S(2)}) copy-start(f32[40,128]{1,0:T(8,128)} %get-tuple-element.20.rhs_ref) | copy-start | bytes 61444
